TPU v7x, 128 devices: a whole 4x4x4 slice. The times are simulated.
128 devices in a mesh: pipe: 4 (over z_hi, core), expert: 32 (over x, y, z_lo).
Axes of the slice: x: 4, y: 4, z: 4 (z_hi: 2, z_lo: 2; z = z_hi * 2 + z_lo), core: 2. Of those that a mesh axis runs over, the one named last changes fastest.
Arguments:
- layer_input: bfloat16 [4, 4096, 7168], P('pipe', 'expert'), may hold values from -6 to 6
- out_grad: bfloat16 [4, 4096, 7168], P('pipe', 'expert'), may hold values from -6 to 6
- route_ids: int32 [4, 4096, 8], P('pipe', 'expert'), may hold values from 0 to 255, as said below
- route_gates: float32 [4, 4096, 8], P('pipe', 'expert'), may hold values from 0.2 to 1.2
- gate_weight: bfloat16 [4, 32, 7168, 256], P('pipe', 'expert'), may hold values from -0.0625 to 0.0625
- up_weight: bfloat16 [4, 32, 7168, 256], P('pipe', 'expert'), may hold values from -0.0625 to 0.0625
- down_weight: bfloat16 [4, 32, 256, 7168], P('pipe', 'expert'), may hold values from -0.125 to 0.125
- head_grad: bfloat16 [4096, 7168], P('expert'), may hold values from -6 to 6
Outputs:
- next_grad: bfloat16 [4, 4096, 7168], P('pipe', 'expert')
- gate_grad: float32 [4, 4096, 8], P('pipe', 'expert')
Inputs may be any that keep to these rules, and one draw needn't show every extreme that they name: `route_ids`: ids of one token are distinct. In each section and in the rows of one device, at most 16 tokens name any one expert below 4; in each section some such expert is named by exactly 16 tokens in the rows of every device.
All inputs are finite; a program needn't handle non-finite values.
Results may differ from a plain program's by a relative error of at most 0.0059.
Values may be sent and summed in bfloat16 or wider, within the bound.
No kernel may reach another device: no remote copies, remote signals or barrier semaphores. Data moves between devices by JAX's collectives and lax.ppermute only.
A program may use at most 128 MiB of HBM per device.

v0:
```python
import jax
import jax.numpy as jnp
from jax import lax
from jax.experimental import pallas as pl
from jax.experimental.pallas import tpu as pltpu
from jax.sharding import PartitionSpec as P

CAP = 16
MARKS = 128
NX, NY, NZ = 4, 4, 2
TIED = ()
FLOPS = 40
BLEND = 25000000000
VMEM = pl.BlockSpec(memory_space=pltpu.VMEM)
SMEM = pl.BlockSpec(memory_space=pltpu.SMEM)
BLOCKS = [(dy, dz) for dz in range(NZ) for dy in range(NY)]
PLUS, MINUS, CROSS = dict(dy=1), dict(dy=-1), dict(dz=1)


def place(x, y, z):
    return ((x % NX) * NY + y % NY) * NZ + z % NZ


def send(block, dx=0, dy=0, dz=0, back=0):
    route = []
    for x in range(NX):
        for y in range(NY):
            for z in range(NZ):
                route.append((place(x, y, z), place(x + dx, y + dy, z + dz)))
    if not back:
        return lax.ppermute(block, "expert", route)
    size = NX * NY * NZ
    route = [
        (p * size + i, (p - back) * size + j)
        for p in range(back, lax.axis_size("pipe"))
        for i, j in route
    ]
    return lax.ppermute(block, ("pipe", "expert"), route)


class Rows:
    def __init__(self, array, start, rows):
        self.array, self.start, self.shape = array, start, (rows, array.shape[1])
        self.dtype = array.dtype

    def __getitem__(self, cut):
        first, last, _ = cut.indices(self.shape[0])
        return Rows(self.array, self.start + first, last - first)

    def value(self):
        if self.shape[0] == self.array.shape[0]:
            return self.array
        return self.array[self.start : self.start + self.shape[0]]


def value(block):
    return block.value() if isinstance(block, Rows) else block


def located(block):
    return (block.array, block.start) if isinstance(block, Rows) else (block, 0)


class Links:
    def __init__(self):
        self.phase = 0
        self.due = {}
        self.queue = {}

    def add(self, block, held, key, lag=1, **hop):
        kind = (tuple(sorted(hop.items())), lag, block.dtype, block.shape[-1])
        group = self.queue.setdefault(kind, [])
        group.append((block, held, key))

    def run(self, others=()):
        groups = list(self.queue.items())
        blocks = [
            jnp.concatenate([value(b) for b, _, _ in moves]) if len(moves) > 1 else value(moves[0][0])
            for _, moves in groups
        ]
        self.last = []
        blocks, _ = lax.optimization_barrier(
            (blocks, self.due.pop(self.phase, []) + list(others))
        )
        for block, ((hop, lag, _, _), moves) in zip(blocks, groups):
            result = send(block, **dict(hop))
            self.due.setdefault(self.phase + lag, []).append(result)
            if lag == 1:
                self.last.append(result)
            start = 0
            for sent, held, key in moves:
                rows = sent.shape[0]
                held[key] = Rows(result, start, rows)
                start += rows
        self.phase += 1
        self.queue = {}


class Spread:
    def __init__(self):
        self.rows, self.ins, self.grads = {}, {}, {}

    def both(self, key):
        self.ins[key], self.grads[key] = self.rows[key][:CAP], self.rows[key][CAP:]

    def first(self, links):
        rows = self.rows
        self.both((0, 0))
        links.add(rows[0, 0], rows, (3, 0), **PLUS)
        links.add(rows[0, 0], rows, (1, 0), **MINUS)
        links.add(rows[0, 0], rows, (0, 1), **CROSS)

    def second(self, links):
        ins, grads = self.ins, self.grads
        for key in ((3, 0), (1, 0), (0, 1)):
            self.both(key)
        links.add(ins[3, 0], ins, (2, 0), **PLUS)
        links.add(ins[0, 1], ins, (3, 1), **PLUS)
        links.add(grads[1, 0], grads, (2, 0), **MINUS)
        links.add(ins[0, 1], ins, (1, 1), **MINUS)
        links.add(grads[1, 0], grads, (1, 1), **CROSS)
        links.add(grads[3, 0], grads, (3, 1), **CROSS)

    def third(self, links):
        links.add(self.ins[3, 1], self.ins, (2, 1), **PLUS)
        links.add(self.grads[1, 1], self.grads, (2, 1), **MINUS)


def added(*parts):
    total = value(parts[0]).astype(jnp.float32)
    for part in parts[1:]:
        total = total + value(part).astype(jnp.float32)
    return total.astype(jnp.bfloat16)


class LateCross:
    def __init__(self, terms):
        self.terms, self.got = terms, {}

    def first(self, links):
        links.add(self.terms[2, 0], self.got, "far+", **PLUS)
        links.add(self.terms[2, 1], self.got, "far-", **MINUS)

    def second(self, links):
        terms, got = self.terms, self.got
        links.add(added(terms[1, 0], got["far+"]), got, "a+", **PLUS)
        links.add(terms[1, 1], got, "b+", **PLUS)
        links.add(terms[3, 0], got, "a-", **MINUS)
        links.add(added(terms[3, 1], got["far-"]), got, "b-", **MINUS)

    def third(self, links):
        got = self.got
        links.add(added(self.terms[0, 1], got["b+"], got["b-"]), got, "z", **CROSS)

    def total(self):
        got = self.got
        return added(self.terms[0, 0], got["a+"], got["a-"], got["z"])


class SoonCross:
    def __init__(self, terms):
        self.terms, self.got = terms, {}

    def first(self, links):
        for dy in range(NY):
            links.add(self.terms[dy, 1], self.got, dy, **CROSS)

    def second(self, links):
        got = self.got
        half = CAP // 2
        self.sums = [added(self.terms[dy, 0], got[dy]) for dy in range(NY)]
        links.add(self.sums[2][:half], got, "far+", **PLUS)
        links.add(self.sums[2][half:], got, "far-", **MINUS)

    def third(self, links):
        sums, got = self.sums, self.got
        half = CAP // 2
        links.add(
            jnp.concatenate([added(sums[1][:half], got["far+"]), sums[1][half:]]),
            got,
            "+",
            **PLUS,
        )
        links.add(
            jnp.concatenate([sums[3][:half], added(sums[3][half:], got["far-"])]),
            got,
            "-",
            **MINUS,
        )

    def total(self):
        return added(self.sums[0], self.got["+"], self.got["-"])


def distinct(pieces):
    arrays = []
    for array, _ in pieces:
        if not any(array is other for other in arrays):
            arrays.append(array)
    return arrays


def index_of(arrays, array):
    return next(i for i, other in enumerate(arrays) if other is array)


def experts_backward(piece, in_pieces, grad_pieces, gate_mat, up_mat, down_mat):
    arrays = distinct(in_pieces + grad_pieces)
    in_plan = [(index_of(arrays, a), r) for a, r in in_pieces]
    grad_plan = [(index_of(arrays, a), r) for a, r in grad_pieces]
    depth, units = gate_mat.shape
    rows = len(in_pieces) * CAP
    step = 1024 if depth % 1024 == 0 else 128

    def kernel(piece_ref, *refs):
        ins = refs[: len(arrays)]
        gate_ref, up_ref, down_ref, out_ref, x_ref, g_ref, a_ref, u_ref, h_ref = refs[
            len(arrays) :
        ]
        a_ref[...] = jnp.zeros_like(a_ref)
        u_ref[...] = jnp.zeros_like(u_ref)
        h_ref[...] = jnp.zeros_like(h_ref)

        @pl.loop(0, depth // step)
        def _(i):
            cols = pl.ds(pl.multiple_of(i * step, step), step)
            for n, (a, r) in enumerate(in_plan):
                x_ref[pl.ds(n * CAP, CAP), :] = ins[a][pl.ds(r, CAP), cols]
            for n, (a, r) in enumerate(grad_plan):
                g_ref[pl.ds(n * CAP, CAP), :] = ins[a][pl.ds(r, CAP), cols]
            x = x_ref[...]
            a_ref[...] += jnp.dot(x, gate_ref[cols, :], preferred_element_type=jnp.float32)
            u_ref[...] += jnp.dot(x, up_ref[cols, :], preferred_element_type=jnp.float32)
            h_ref[...] += lax.dot_general(
                g_ref[...],
                down_ref[:, cols],
                (((1,), (1,)), ((), ())),
                preferred_element_type=jnp.float32,
            )

        gate_pre, up_pre, hidden_grad = a_ref[...], u_ref[...], h_ref[...]
        sigma = jax.nn.sigmoid(gate_pre)
        swish = gate_pre * sigma
        score = jnp.sum(swish * up_pre * hidden_grad, axis=1, keepdims=True)
        gate_back = (hidden_grad * up_pre * sigma * (1.0 + gate_pre * (1.0 - sigma))).astype(
            jnp.bfloat16
        )
        up_back = (hidden_grad * swish).astype(jnp.bfloat16)
        lane = lax.broadcasted_iota(jnp.int32, (rows, MARKS), 1)
        marks = jnp.where(lane == piece_ref[0], score, 0.0)
        out_ref[:, pl.ds(depth, MARKS)] = marks.astype(jnp.bfloat16)

        @pl.loop(0, depth // step)
        def _(i):
            cols = pl.ds(pl.multiple_of(i * step, step), step)
            term = lax.dot_general(
                gate_back,
                gate_ref[cols, :],
                (((1,), (1,)), ((), ())),
                preferred_element_type=jnp.float32,
            )
            term = term + lax.dot_general(
                up_back,
                up_ref[cols, :],
                (((1,), (1,)), ((), ())),
                preferred_element_type=jnp.float32,
            )
            out_ref[:, cols] = term.astype(jnp.bfloat16)

    return pl.pallas_call(
        kernel,
        out_shape=jax.ShapeDtypeStruct((rows, depth + MARKS), jnp.bfloat16),
        in_specs=[SMEM] + [VMEM] * (len(arrays) + 3),
        out_specs=VMEM,
        scratch_shapes=[
            pltpu.VMEM((rows, step), jnp.bfloat16),
            pltpu.VMEM((rows, step), jnp.bfloat16),
            pltpu.VMEM((rows, units), jnp.float32),
            pltpu.VMEM((rows, units), jnp.float32),
            pltpu.VMEM((rows, units), jnp.float32),
        ],
        cost_estimate=pl.CostEstimate(
            flops=FLOPS * rows * depth * units,
            bytes_accessed=2 * (3 * depth * units + 3 * rows * depth),
            transcendentals=rows * units,
        ),
    )(piece, *arrays, gate_mat, up_mat, down_mat)


def blend(base, mix, rows):
    tokens, width = base.shape
    step = 1024 if width % 1024 == 0 else 128

    def kernel(base_ref, mix_ref, *refs):
        out_ref = refs[-1]
        total = base_ref[...].astype(jnp.float32)
        for n, row_ref in enumerate(refs[:-1]):
            weight = mix_ref[:, n * CAP : (n + 1) * CAP]
            high = weight.astype(jnp.bfloat16)
            low = (weight - high.astype(jnp.float32)).astype(jnp.bfloat16)
            for part in (high, low):
                total = total + jnp.dot(part, row_ref[...], preferred_element_type=jnp.float32)
        out_ref[...] = total

    return pl.pallas_call(
        kernel,
        grid=(width // step,),
        out_shape=jax.ShapeDtypeStruct((tokens, width), jnp.float32),
        in_specs=[
            pl.BlockSpec((tokens, step), lambda i: (0, i)),
            pl.BlockSpec(mix.shape, lambda i: (0, 0)),
        ]
        + [pl.BlockSpec((CAP, step), lambda i: (0, i))] * len(rows),
        out_specs=pl.BlockSpec((tokens, step), lambda i: (0, i)),
        cost_estimate=pl.CostEstimate(flops=BLEND, bytes_accessed=8 * tokens * width, transcendentals=0),
    )(base, mix, *rows)


def body(
    layer_input, out_grad, route_ids, route_gates, gate_weight, up_weight, down_weight, head_grad
):
    holder = lax.axis_index("expert")
    group = holder // (NY * NZ)
    piece = (holder % (NY * NZ)).astype(jnp.int32).reshape(1)
    tokens = layer_input[0]
    width = tokens.shape[1]
    grads = out_grad[0]
    routes = route_ids[0]
    gates = route_gates[0]
    weights = gate_weight[0, 0], up_weight[0, 0], down_weight[0, 0]
    order = (jnp.arange(NX, dtype=jnp.int32) + group) % NX
    named = routes[:, :, None] == order[None, None, :]
    hits = jnp.any(named, axis=1).astype(jnp.int32)
    places = jnp.cumsum(hits, axis=0) - hits
    chosen = (places[:, :, None] == jnp.arange(CAP, dtype=jnp.int32)) & (hits[:, :, None] == 1)
    picker = chosen.astype(jnp.bfloat16)
    token_rows = jnp.einsum(
        "tec,td->ecd", picker, tokens, preferred_element_type=jnp.float32
    ).astype(jnp.bfloat16)
    grad_rows = jnp.einsum("tec,td->ecd", picker, grads, preferred_element_type=jnp.float32).astype(
        jnp.bfloat16
    )
    weighted_gate = jnp.sum(gates[:, :, None] * named.astype(jnp.float32), axis=1)
    chosen_float = chosen.astype(jnp.float32)
    mixing = (chosen_float * weighted_gate[:, :, None]).reshape(-1, NX * CAP)

    units = [Spread() for _ in range(NX)]
    rows = [jnp.concatenate([token_rows[dx], grad_rows[dx]]) for dx in range(NX)]
    back, moved, scores = {}, {}, {}
    units[0].rows[0, 0] = Rows(rows[0], 0, 2 * CAP)
    for dx in (1, 3):
        units[dx].rows[0, 0] = Rows(send(rows[dx], dx=dx), 0, 2 * CAP)

    def compute(dxs, kinds):
        ins = [located(units[dx].ins[k]) for dx in dxs for k in BLOCKS]
        gs = [located(units[dx].grads[k]) for dx in dxs for k in BLOCKS]
        term = experts_backward(piece, ins, gs, *weights)
        term = term.reshape(len(dxs), len(BLOCKS), CAP, -1)
        return [
            kind({k: term[i, n] for n, k in enumerate(BLOCKS)}) for i, kind in enumerate(kinds)
        ]

    def home(links, dx, reduced):
        part = reduced.total()
        marks = part[:, width:]
        if dx:
            links.add(marks, scores, dx, dx=-dx)
        else:
            scores[dx] = marks
        links.add(part[:, :width], moved, dx, dx=-dx, back=1)

    def chain(dxs):
        links = Links()
        one, two = (units[dx] for dx in dxs)
        one.first(links)
        if 2 in dxs:
            links.add(rows[2], units[2].rows, (0, 0), dx=2)
        yield links
        two.first(links)
        one.second(links)
        if 0 in dxs:
            links.add(grads, back, "grads", lag=3, back=1)
            links.add(mixing, back, "mixing", lag=3, back=1)
        yield links
        two.second(links)
        one.third(links)
        yield links
        two.third(links)
        yield links
        sums = compute(dxs, [LateCross, SoonCross])
        for part in sums:
            part.first(links)
        yield links
        for part in sums:
            part.second(links)
        yield links
        for part in sums:
            part.third(links)
        yield links
        for dx, part in zip(dxs, sums):
            home(links, dx, part)
        yield links

    for phase, (early, late) in enumerate(zip(chain((0, 1)), chain((3, 2)))):
        early.run()
        late.run(early.last if phase in TIED else ())

    mix = value(back["mixing"])
    early = blend(value(back["grads"]), mix[:, : 2 * CAP], [value(moved[dx]) for dx in (0, 1)])
    sums = jnp.concatenate([value(moved[dx]) for dx in (2, 3)])
    mix = mix[:, 2 * CAP :]
    high = lax.reduce_precision(mix, 8, 7)
    moe_grad = jnp.dot(
        high.astype(jnp.bfloat16), sums, preferred_element_type=jnp.float32
    ) + jnp.dot((mix - high).astype(jnp.bfloat16), sums, preferred_element_type=jnp.float32)
    passed = (early + moe_grad).astype(jnp.bfloat16)
    last_section = lax.axis_index("pipe") == lax.axis_size("pipe") - 1
    next_grad = jnp.where(last_section, head_grad, passed)

    totals = jnp.sum(jnp.stack([value(scores[dx]) for dx in range(NX)]).astype(jnp.float32), axis=2)
    token_scores = jnp.sum(chosen_float * totals[None], axis=2)
    gate_grad = jnp.sum(named.astype(jnp.float32) * token_scores[:, None, :], axis=2)
    return (next_grad[None], gate_grad[None])


def solution(mesh):
    in_specs = (
        P("pipe", "expert", None),
        P("pipe", "expert", None),
        P("pipe", "expert", None),
        P("pipe", "expert", None),
        P("pipe", "expert", None, None),
        P("pipe", "expert", None, None),
        P("pipe", "expert", None, None),
        P("expert", None),
    )
    out_specs = (P("pipe", "expert", None), P("pipe", "expert", None))
    return jax.shard_map(body, mesh=mesh, in_specs=in_specs, out_specs=out_specs, check_vma=False)
```

profile of v0, /device:TPU:1, one launch (start us, length us, event | category | flops | bytes accessed | tf_op | source)
XLA Modules:
  0.0 234.1 jit_solution(645253184057162920)
XLA Ops:
  0.7 0.9 compare_reduce_fusion
  2.6 1.0 copy-done.5
  4.2 3.4 %collective-permute-start.24 = (bf16[32,7168]{1,0:T(8,128)(2,1)S(1)}, bf16[32,7168]{1,0:T(8,128)(2,1)}, u32[]{:S(2)}, u32[]{:S(2)}) collective-permute-start(bf16[32,7168]{1,0:T(8,128)(2,1)S(1)} %pad_maximum_fusion.23), channel_id=1, source_target_pairs={{0,24},{1,25},{2,26},{3,27},{4,28},{5,29},{6,30},{7,31},{8,0},{9,1... | collective-permute-start | bytes 1376264 | tf_op jit(solution)/shard_map/ppermute | solution.py:31
  7.6 1.4 collective-permute-start.1
  9.0 1.6 collective-permute-start.2
  10.6 1.5 collective-permute-start.3
  12.9 3.9 %collective-permute-done.24.refs_0_ = bf16[32,7168]{1,0:T(8,128)(2,1)} collective-permute-done((bf16[32,7168]{1,0:T(8,128)(2,1)S(1)}, bf16[32,7168]{1,0:T(8,128)(2,1)}, u32[]{:S(2)}, u32[]{:S(2)}) %collective-permute-start.24) | collective-permute-done | bytes 458784 | tf_op jit(solution)/shard_map/ppermute | solution.py:31
  16.8 1.3 collective-permute-start.27
  18.0 2.1 collective-permute-done.1.refs_3_
  20.1 1.7 collective-permute-start.28
  21.8 1.6 collective-permute-start.25
  23.4 1.0 slice.437
  24.9 1.0 slice.438
  26.7 3.2 %collective-permute-done.27.refs_3_ = bf16[32,7168]{1,0:T(8,128)(2,1)S(1)} collective-permute-done((bf16[32,7168]{1,0:T(8,128)(2,1)}, bf16[32,7168]{1,0:T(8,128)(2,1)S(1)}, u32[]{:S(2)}, u32[]{:S(2)}) %collective-permute-start.27) | collective-permute-done | bytes 458784 | tf_op jit(solution)/shard_map/ppermute | solution.py:31
  29.9 1.4 collective-permute-start.7
  31.4 1.7 collective-permute-start.8
  33.2 2.0 collective-permute-done.26.refs_7_
  35.9 2.7 %collective-permute-start.30 = (bf16[64,7168]{1,0:T(8,128)(2,1)S(1)}, bf16[64,7168]{1,0:T(8,128)(2,1)S(1)}, u32[]{:S(2)}, u32[]{:S(2)}) collective-permute-start(bf16[64,7168]{1,0:T(8,128)(2,1)S(1)} %get-tuple-element.78), channel_id=1, source_target_pairs={{0,6},{1,7},{2,0},{3,1},{4,2},{5,3},{6,4},{7,5},{8,14},{9,15},{10,... | collective-permute-start | bytes 2752520 | tf_op jit(solution)/shard_map/ppermute | solution.py:31
  38.6 13.8 %collective-permute-done.7.refs_5_ = bf16[64,7168]{1,0:T(8,128)(2,1)S(1)} collective-permute-done((bf16[64,7168]{1,0:T(8,128)(2,1)S(1)}, bf16[64,7168]{1,0:T(8,128)(2,1)S(1)}, u32[]{:S(2)}, u32[]{:S(2)}) %collective-permute-start.7) | collective-permute-done | bytes 917536 | tf_op jit(solution)/shard_map/ppermute | solution.py:31
  52.5 0.7 copy-done.24
  53.9 2.6 %collective-permute-start.10 = (bf16[48,7168]{1,0:T(8,128)(2,1)S(1)}, bf16[48,7168]{1,0:T(8,128)(2,1)S(1)}, u32[]{:S(2)}, u32[]{:S(2)}) collective-permute-start(bf16[48,7168]{1,0:T(8,128)(2,1)S(1)} %get-tuple-element.59), channel_id=1, source_target_pairs={{0,6},{1,7},{2,0},{3,1},{4,2},{5,3},{6,4},{7,5},{8,14},{9,15},{10,... | collective-permute-start | bytes 2064392 | tf_op jit(solution)/shard_map/ppermute | solution.py:31
  56.6 15.4 %collective-permute-done.30.refs_5_ = bf16[64,7168]{1,0:T(8,128)(2,1)S(1)} collective-permute-done((bf16[64,7168]{1,0:T(8,128)(2,1)S(1)}, bf16[64,7168]{1,0:T(8,128)(2,1)S(1)}, u32[]{:S(2)}, u32[]{:S(2)}) %collective-permute-start.30) | collective-permute-done | bytes 917536 | tf_op jit(solution)/shard_map/ppermute | solution.py:31
  73.5 1.2 collective-permute-start.34
  74.8 4.9 %collective-permute-done.11.refs_11_ = bf16[32,7168]{1,0:T(8,128)(2,1)S(1)} collective-permute-done((bf16[32,7168]{1,0:T(8,128)(2,1)S(1)}, bf16[32,7168]{1,0:T(8,128)(2,1)S(1)}, u32[]{:S(2)}, u32[]{:S(2)}) %collective-permute-start.11) | collective-permute-done | bytes 458784 | tf_op jit(solution)/shard_map/ppermute | solution.py:31
  79.7 3.3 %collective-permute-done.9.refs_6_ = bf16[48,7168]{1,0:T(8,128)(2,1)S(1)} collective-permute-done((bf16[48,7168]{1,0:T(8,128)(2,1)S(1)}, bf16[48,7168]{1,0:T(8,128)(2,1)S(1)}, u32[]{:S(2)}, u32[]{:S(2)}) %collective-permute-start.9) | collective-permute-done | bytes 688160 | tf_op jit(solution)/shard_map/ppermute | solution.py:31
  83.0 3.7 %collective-permute-done.10.refs_9_ = bf16[48,7168]{1,0:T(8,128)(2,1)S(1)} collective-permute-done((bf16[48,7168]{1,0:T(8,128)(2,1)S(1)}, bf16[48,7168]{1,0:T(8,128)(2,1)S(1)}, u32[]{:S(2)}, u32[]{:S(2)}) %collective-permute-start.10) | collective-permute-done | bytes 688160 | tf_op jit(solution)/shard_map/ppermute | solution.py:31
  86.8 0.8 copy-done.27
  87.6 2.6 %collective-permute-start.13 = (bf16[16,7168]{1,0:T(8,128)(2,1)S(1)}, bf16[16,7168]{1,0:T(8,128)(2,1)}, u32[]{:S(2)}, u32[]{:S(2)}) collective-permute-start(bf16[16,7168]{1,0:T(8,128)(2,1)S(1)} %slice.448), channel_id=1, source_target_pairs={{0,6},{1,7},{2,0},{3,1},{4,2},{5,3},{6,4},{7,5},{8,14},{9,15},{10,... | collective-permute-start | bytes 688136 | tf_op jit(solution)/shard_map/ppermute | solution.py:31
  90.2 5.7 %collective-permute-start.4 = (bf16[128,7168]{1,0:T(8,128)(2,1)}, bf16[128,7168]{1,0:T(8,128)(2,1)}, u32[]{:S(2)}, u32[]{:S(2)}) collective-permute-start(bf16[128,7168]{1,0:T(8,128)(2,1)} %bitcast.166), channel_id=1, source_target_pairs={{32,0},{33,1},{34,2},{35,3},{36,4},{37,5},{38,6},{39,7},{40,8},{41... | collective-permute-start | bytes 5505032 | tf_op jit(solution)/shard_map/ppermute | solution.py:38
  95.9 1.9 collective-permute-start.5
  98.0 2.9 %collective-permute-start.33 = (bf16[48,7168]{1,0:T(8,128)(2,1)S(1)}, bf16[48,7168]{1,0:T(8,128)(2,1)}, u32[]{:S(2)}, u32[]{:S(2)}) collective-permute-start(bf16[48,7168]{1,0:T(8,128)(2,1)S(1)} %get-tuple-element.81), channel_id=1, source_target_pairs={{0,6},{1,7},{2,0},{3,1},{4,2},{5,3},{6,4},{7,5},{8,14},{9,15},{10,... | collective-permute-start | bytes 2064392 | tf_op jit(solution)/shard_map/ppermute | solution.py:31
  100.9 15.8 %shard_map.95 = bf16[256,7296]{1,0:T(8,128)(2,1)} custom-call(s32[1]{0:T(128)} %bitcast.13.piece_ref, bf16[32,7168]{1,0:T(8,128)(2,1)} %copy-done.9, bf16[32,7168]{1,0:T(8,128)(2,1)} %collective-permute-done.3.refs_1_, bf16[64,7168]{1,0:T(8,128)(2,1)} %copy-done.8, bf16[32,7168]{1,0:T(8,128)(2,1)} %copy-done.11, ...), custom_call_target="tpu_custom_call" | custom-call | flops 18790481920 | bytes 22020096 | tf_op jit(solution)/shard_map/pallas_call | solution.py:270
  116.7 2.4 %slice_bitcast_fusion.21 = (bf16[16,7296]{1,0:T(8,128)(2,1)S(1)}, bf16[16,7296]{1,0:T(8,128)(2,1)S(1)}, bf16[16,7296]{1,0:T(8,128)(2,1)S(1)}, bf16[16,7296]{1,0:...) fusion(bf16[2,8,16,7296]{3,2,1,0:T(8,128)(2,1)} %bitcast.158), kind=kLoop, calls=%fused_computation.99 | loop fusion | bytes 3735552 | tf_op jit(solution)/shard_map/squeeze | solution.py:360
  119.1 1.0 slice.499
  120.1 2.7 %collective-permute-start.36 = (bf16[16,7168]{1,0:T(8,128)(2,1)S(1)}, bf16[16,7168]{1,0:T(8,128)(2,1)}, u32[]{:S(2)}, u32[]{:S(2)}) collective-permute-start(bf16[16,7168]{1,0:T(8,128)(2,1)S(1)} %slice.500), channel_id=1, source_target_pairs={{0,6},{1,7},{2,0},{3,1},{4,2},{5,3},{6,4},{7,5},{8,14},{9,15},{10,... | collective-permute-start | bytes 688136 | tf_op jit(solution)/shard_map/ppermute | solution.py:31
  122.8 1.0 pad_maximum_fusion.8
  124.0 2.7 %collective-permute-start.16 = (bf16[16,7296]{1,0:T(8,128)(2,1)S(1)}, bf16[16,7296]{1,0:T(8,128)(2,1)}, u32[]{:S(2)}, u32[]{:S(2)}) collective-permute-start(bf16[16,7296]{1,0:T(8,128)(2,1)S(1)} %get-tuple-element.65), channel_id=1, source_target_pairs={{0,6},{1,7},{2,0},{3,1},{4,2},{5,3},{6,4},{7,5},{8,14},{9,15},{10,... | collective-permute-start | bytes 700424 | tf_op jit(solution)/shard_map/ppermute | solution.py:31
  126.7 2.2 collective-permute-done.35.refs_10_
  128.9 0.7 copy-done.30
  129.6 15.7 %shard_map.97 = bf16[256,7296]{1,0:T(8,128)(2,1)} custom-call(s32[1]{0:T(128)} %bitcast.13.piece_ref, bf16[32,7168]{1,0:T(8,128)(2,1)} %collective-permute-done.24.refs_0_, bf16[32,7168]{1,0:T(8,128)(2,1)} %copy-done.19, bf16[64,7168]{1,0:T(8,128)(2,1)} %copy-done.7, bf16[32,7168]{1,0:T(8,128)(2,1)} %copy-done.10, bf16[32,7168]{1,0:T(8,128)(2,1)} %copy-done.18, ...), custom_call_target="tpu_custom_call" | custom-call | flops 18790481920 | bytes 22020096 | tf_op jit(solution)/shard_map/pallas_call | solution.py:270
  145.3 1.8 slice_bitcast_fusion.5
  147.4 2.7 %collective-permute-start.39 = (bf16[16,7296]{1,0:T(8,128)(2,1)S(1)}, bf16[16,7296]{1,0:T(8,128)(2,1)S(1)}, u32[]{:S(2)}, u32[]{:S(2)}) collective-permute-start(bf16[16,7296]{1,0:T(8,128)(2,1)S(1)} %get-tuple-element.87), channel_id=1, source_target_pairs={{0,6},{1,7},{2,0},{3,1},{4,2},{5,3},{6,4},{7,5},{8,14},{9,15},{10,... | collective-permute-start | bytes 700424 | tf_op jit(solution)/shard_map/ppermute | solution.py:31
  150.1 1.5 fusion.20
  151.7 1.0 collective-permute-start.18
  153.4 2.3 collective-permute-done.37
  155.7 13.9 %collective-permute-done.38 = bf16[64,7296]{1,0:T(8,128)(2,1)S(1)} collective-permute-done((bf16[64,7296]{1,0:T(8,128)(2,1)S(1)}, bf16[64,7296]{1,0:T(8,128)(2,1)S(1)}, u32[]{:S(2)}, u32[]{:S(2)}) %collective-permute-start.38) | collective-permute-done | bytes 933920 | tf_op jit(solution)/shard_map/ppermute | solution.py:31
  170.0 1.7 collective-permute-start.41
  172.2 2.7 %collective-permute-start.21 = (bf16[16,7296]{1,0:T(8,128)(2,1)S(1)}, bf16[16,7296]{1,0:T(8,128)(2,1)S(1)}, u32[]{:S(2)}, u32[]{:S(2)}) collective-permute-start(bf16[16,7296]{1,0:T(8,128)(2,1)S(1)} %pad_maximum_fusion.27), channel_id=1, source_target_pairs={{0,6},{1,7},{2,0},{3,1},{4,2},{5,3},{6,4},{7,5},{8,14},{9,15},{10,... | collective-permute-start | bytes 700424 | tf_op jit(solution)/shard_map/ppermute | solution.py:31
  174.9 9.0 %collective-permute-done.41 = bf16[40,7296]{1,0:T(8,128)(2,1)S(1)} collective-permute-done((bf16[40,7296]{1,0:T(8,128)(2,1)S(1)}, bf16[40,7296]{1,0:T(8,128)(2,1)S(1)}, u32[]{:S(2)}, u32[]{:S(2)}) %collective-permute-start.41) | collective-permute-done | bytes 583712 | tf_op jit(solution)/shard_map/ppermute | solution.py:31
  184.0 2.0 collective-permute-done.40
  186.4 2.7 %collective-permute-start.44 = (bf16[16,7296]{1,0:T(8,128)(2,1)S(1)}, bf16[16,7296]{1,0:T(8,128)(2,1)S(1)}, u32[]{:S(2)}, u32[]{:S(2)}) collective-permute-start(bf16[16,7296]{1,0:T(8,128)(2,1)S(1)} %pad_maximum_fusion.29), channel_id=1, source_target_pairs={{0,6},{1,7},{2,0},{3,1},{4,2},{5,3},{6,4},{7,5},{8,14},{9,15},{10,... | collective-permute-start | bytes 700424 | tf_op jit(solution)/shard_map/ppermute | solution.py:31
  189.1 1.9 collective-permute-done.20
  191.3 0.8 collective-permute-start.47
  192.1 7.0 %collective-permute-start.22 = (bf16[16,7168]{1,0:T(8,128)(2,1)S(1)}, bf16[16,7168]{1,0:T(8,128)(2,1)S(1)}, u32[]{:S(2)}, u32[]{:S(2)}) collective-permute-start(bf16[16,7168]{1,0:T(8,128)(2,1)S(1)} %slice.479), channel_id=1, source_target_pairs={{32,0},{33,1},{34,2},{35,3},{36,4},{37,5},{38,6},{39,7},{40,8},{41... | collective-permute-start | bytes 688136 | tf_op jit(solution)/shard_map/ppermute | solution.py:38
  199.1 1.9 collective-permute-start.23
  201.4 1.8 collective-permute-start.48
  203.2 1.8 collective-permute-done.22.refs_0_
  205.0 1.9 collective-permute-start.45
  206.9 3.4 %collective-permute-done.23.refs_1_ = bf16[16,7168]{1,0:T(8,128)(2,1)S(1)} collective-permute-done((bf16[16,7168]{1,0:T(8,128)(2,1)S(1)}, bf16[16,7168]{1,0:T(8,128)(2,1)S(1)}, u32[]{:S(2)}, u32[]{:S(2)}) %collective-permute-start.23) | collective-permute-done | bytes 229408 | tf_op jit(solution)/shard_map/ppermute | solution.py:38
  211.0 7.0 %shard_map.96 = f32[128,7168]{1,0:T(8,128)} custom-call(bf16[128,7168]{1,0:T(8,128)(2,1)} %collective-permute-done.4.base_ref, f32[128,32]{1,0:T(8,128)} %bitcast.167, bf16[16,7168]{1,0:T(8,128)(2,1)} %copy-done.29, bf16[16,7168]{1,0:T(8,128)(2,1)} %copy-done.31), custom_call_target="tpu_custom_call" | custom-call | flops 24999999488 | bytes 7340032 | tf_op jit(solution)/shard_map/pallas_call | solution.py:305
  218.0 1.9 collective-permute-start.46
  220.9 8.1 %collective-permute-done.46 = bf16[16,7168]{1,0:T(8,128)(2,1)S(1)} collective-permute-done((bf16[16,7168]{1,0:T(8,128)(2,1)S(1)}, bf16[16,7168]{1,0:T(8,128)(2,1)S(1)}, u32[]{:S(2)}, u32[]{:S(2)}) %collective-permute-start.46) | collective-permute-done | bytes 229408 | tf_op jit(solution)/shard_map/ppermute | solution.py:38
  230.4 1.3 copy-done.4
  232.3 1.8 fusion.1
  (193 shorter events, 13.6 us)
Async XLA Ops:
  4.1 8.4 %copy-start.25 = (s32[1,128,8]{1,2,0:T(8,128)S(1)}, s32[1,128,8]{1,2,0:T(8,128)}, u32[]{:S(2)}) copy-start(s32[1,128,8]{1,2,0:T(8,128)} %param.10) | copy-start | bytes 12292
  4.1 8.4 %copy-start.26 = (f32[1,128,8]{1,2,0:T(8,128)S(1)}, f32[1,128,8]{1,2,0:T(8,128)}, u32[]{:S(2)}) copy-start(f32[1,128,8]{1,2,0:T(8,128)} %param.11) | copy-start | bytes 12292
  4.2 12.6 %collective-permute-start.24 = (bf16[32,7168]{1,0:T(8,128)(2,1)S(1)}, bf16[32,7168]{1,0:T(8,128)(2,1)}, u32[]{:S(2)}, u32[]{:S(2)}) collective-permute-start(bf16[32,7168]{1,0:T(8,128)(2,1)S(1)} %pad_maximum_fusion.23), channel_id=1, source_target_pairs={{0,24},{1,25},{2,26},{3,27},{4,28},{5,29},{6,30},{7,31},{8,0},{9,1... | collective-permute-start | bytes 1376264 | tf_op jit(solution)/shard_map/ppermute | solution.py:31
  7.6 18.5 %copy-start.9 = (bf16[32,7168]{1,0:T(8,128)(2,1)}, bf16[32,7168]{1,0:T(8,128)(2,1)S(1)}, u32[]{:S(2)}) copy-start(bf16[32,7168]{1,0:T(8,128)(2,1)S(1)} %get-tuple-element.51.refs_0_) | copy-start | bytes 1376260
  7.6 12.5 %collective-permute-start.1 = (bf16[32,7168]{1,0:T(8,128)(2,1)S(1)}, bf16[32,7168]{1,0:T(8,128)(2,1)S(1)}, u32[]{:S(2)}, u32[]{:S(2)}) collective-permute-start(bf16[32,7168]{1,0:T(8,128)(2,1)S(1)} %get-tuple-element.51.refs_0_), channel_id=1, source_target_pairs={{0,2},{1,3},{2,4},{3,5},{4,6},{5,7},{6,0},{7,1},{8,10},{9,11},{10,... | collective-permute-start | bytes 1376264 | tf_op jit(solution)/shard_map/ppermute | solution.py:31
  9.0 12.8 %collective-permute-start.2 = (bf16[32,7168]{1,0:T(8,128)(2,1)S(1)}, bf16[32,7168]{1,0:T(8,128)(2,1)}, u32[]{:S(2)}, u32[]{:S(2)}) collective-permute-start(bf16[32,7168]{1,0:T(8,128)(2,1)S(1)} %get-tuple-element.51.refs_0_), channel_id=1, source_target_pairs={{0,1},{1,0},{2,3},{3,2},{4,5},{5,4},{6,7},{7,6},{8,9},{9,8},{10,11... | collective-permute-start | bytes 1376264 | tf_op jit(solution)/shard_map/ppermute | solution.py:31
  10.6 13.7 %collective-permute-start.3 = (bf16[32,7168]{1,0:T(8,128)(2,1)S(1)}, bf16[32,7168]{1,0:T(8,128)(2,1)}, u32[]{:S(2)}, u32[]{:S(2)}) collective-permute-start(bf16[32,7168]{1,0:T(8,128)(2,1)S(1)} %get-tuple-element.51.refs_0_), channel_id=1, source_target_pairs={{0,6},{1,7},{2,0},{3,1},{4,2},{5,3},{6,4},{7,5},{8,14},{9,15},{10,... | collective-permute-start | bytes 1376264 | tf_op jit(solution)/shard_map/ppermute | solution.py:31
  12.2 13.7 %collective-permute-start = (bf16[32,7168]{1,0:T(8,128)(2,1)S(1)}, bf16[32,7168]{1,0:T(8,128)(2,1)S(1)}, u32[]{:S(2)}, u32[]{:S(2)}) collective-permute-start(bf16[32,7168]{1,0:T(8,128)(2,1)S(1)} %pad_maximum_fusion.20), channel_id=1, source_target_pairs={{0,8},{1,9},{2,10},{3,11},{4,12},{5,13},{6,14},{7,15},{8,16},{9,17... | collective-permute-start | bytes 1376264 | tf_op jit(solution)/shard_map/ppermute | solution.py:31
  16.8 13.2 %collective-permute-start.27 = (bf16[32,7168]{1,0:T(8,128)(2,1)}, bf16[32,7168]{1,0:T(8,128)(2,1)S(1)}, u32[]{:S(2)}, u32[]{:S(2)}) collective-permute-start(bf16[32,7168]{1,0:T(8,128)(2,1)} %collective-permute-done.24.refs_0_), channel_id=1, source_target_pairs={{0,2},{1,3},{2,4},{3,5},{4,6},{5,7},{6,0},{7,1},{8,10},{9,11},{10,... | collective-permute-start | bytes 1376264 | tf_op jit(solution)/shard_map/ppermute | solution.py:31
  20.1 11.2 %collective-permute-start.28 = (bf16[32,7168]{1,0:T(8,128)(2,1)}, bf16[32,7168]{1,0:T(8,128)(2,1)S(1)}, u32[]{:S(2)}, u32[]{:S(2)}) collective-permute-start(bf16[32,7168]{1,0:T(8,128)(2,1)} %collective-permute-done.24.refs_0_), channel_id=1, source_target_pairs={{0,1},{1,0},{2,3},{3,2},{4,5},{5,4},{6,7},{7,6},{8,9},{9,8},{10,11... | collective-permute-start | bytes 1376264 | tf_op jit(solution)/shard_map/ppermute | solution.py:31
  21.8 11.3 %collective-permute-start.25 = (bf16[32,7168]{1,0:T(8,128)(2,1)}, bf16[32,7168]{1,0:T(8,128)(2,1)S(1)}, u32[]{:S(2)}, u32[]{:S(2)}) collective-permute-start(bf16[32,7168]{1,0:T(8,128)(2,1)} %collective-permute-done.24.refs_0_), channel_id=1, source_target_pairs={{0,6},{1,7},{2,0},{3,1},{4,2},{5,3},{6,4},{7,5},{8,14},{9,15},{10,... | collective-permute-start | bytes 1376264 | tf_op jit(solution)/shard_map/ppermute | solution.py:31
  24.4 10.8 %collective-permute-start.26 = (bf16[32,7168]{1,0:T(8,128)(2,1)S(1)}, bf16[32,7168]{1,0:T(8,128)(2,1)S(1)}, u32[]{:S(2)}, u32[]{:S(2)}) collective-permute-start(bf16[32,7168]{1,0:T(8,128)(2,1)S(1)} %get-tuple-element.74), channel_id=1, source_target_pairs={{0,16},{1,17},{2,18},{3,19},{4,20},{5,21},{6,22},{7,23},{8,24},{9,... | collective-permute-start | bytes 1376264 | tf_op jit(solution)/shard_map/ppermute | solution.py:31
  26.7 25.7 %collective-permute-start.6 = (bf16[64,7168]{1,0:T(8,128)(2,1)S(1)}, bf16[64,7168]{1,0:T(8,128)(2,1)S(1)}, u32[]{:S(2)}, u32[]{:S(2)}) collective-permute-start(bf16[64,7168]{1,0:T(8,128)(2,1)S(1)} %get-tuple-element.55), channel_id=1, source_target_pairs={{0,2},{1,3},{2,4},{3,5},{4,6},{5,7},{6,0},{7,1},{8,10},{9,11},{10,... | collective-permute-start | bytes 2752520 | tf_op jit(solution)/shard_map/ppermute | solution.py:31
  29.9 5.2 %copy-start.10 = (bf16[32,7168]{1,0:T(8,128)(2,1)}, bf16[32,7168]{1,0:T(8,128)(2,1)S(1)}, u32[]{:S(2)}) copy-start(bf16[32,7168]{1,0:T(8,128)(2,1)S(1)} %collective-permute-done.27.refs_3_) | copy-start | bytes 1376260
  29.9 22.4 %collective-permute-start.7 = (bf16[64,7168]{1,0:T(8,128)(2,1)S(1)}, bf16[64,7168]{1,0:T(8,128)(2,1)S(1)}, u32[]{:S(2)}, u32[]{:S(2)}) collective-permute-start(bf16[64,7168]{1,0:T(8,128)(2,1)S(1)} %get-tuple-element.56), channel_id=1, source_target_pairs={{0,6},{1,7},{2,0},{3,1},{4,2},{5,3},{6,4},{7,5},{8,14},{9,15},{10,... | collective-permute-start | bytes 2752520 | tf_op jit(solution)/shard_map/ppermute | solution.py:31
  31.4 3.8 %copy-start.18 = (bf16[32,7168]{1,0:T(8,128)(2,1)}, bf16[32,7168]{1,0:T(8,128)(2,1)S(1)}, u32[]{:S(2)}) copy-start(bf16[32,7168]{1,0:T(8,128)(2,1)S(1)} %collective-permute-done.28.refs_4_) | copy-start | bytes 1376260
  31.4 21.1 %collective-permute-start.8 = (bf16[64,7168]{1,0:T(8,128)(2,1)S(1)}, bf16[64,7168]{1,0:T(8,128)(2,1)S(1)}, u32[]{:S(2)}, u32[]{:S(2)}) collective-permute-start(bf16[64,7168]{1,0:T(8,128)(2,1)S(1)} %get-tuple-element.57), channel_id=1, source_target_pairs={{0,1},{1,0},{2,3},{3,2},{4,5},{5,4},{6,7},{7,6},{8,9},{9,8},{10,11... | collective-permute-start | bytes 2752520 | tf_op jit(solution)/shard_map/ppermute | solution.py:31
  35.9 36.1 %collective-permute-start.29 = (bf16[64,7168]{1,0:T(8,128)(2,1)S(1)}, bf16[64,7168]{1,0:T(8,128)(2,1)S(1)}, u32[]{:S(2)}, u32[]{:S(2)}) collective-permute-start(bf16[64,7168]{1,0:T(8,128)(2,1)S(1)} %get-tuple-element.77), channel_id=1, source_target_pairs={{0,2},{1,3},{2,4},{3,5},{4,6},{5,7},{6,0},{7,1},{8,10},{9,11},{10,... | collective-permute-start | bytes 2752520 | tf_op jit(solution)/shard_map/ppermute | solution.py:31
  35.9 36.1 %collective-permute-start.30 = (bf16[64,7168]{1,0:T(8,128)(2,1)S(1)}, bf16[64,7168]{1,0:T(8,128)(2,1)S(1)}, u32[]{:S(2)}, u32[]{:S(2)}) collective-permute-start(bf16[64,7168]{1,0:T(8,128)(2,1)S(1)} %get-tuple-element.78), channel_id=1, source_target_pairs={{0,6},{1,7},{2,0},{3,1},{4,2},{5,3},{6,4},{7,5},{8,14},{9,15},{10,... | collective-permute-start | bytes 2752520 | tf_op jit(solution)/shard_map/ppermute | solution.py:31
  52.3 19.8 %collective-permute-start.31 = (bf16[64,7168]{1,0:T(8,128)(2,1)S(1)}, bf16[64,7168]{1,0:T(8,128)(2,1)S(1)}, u32[]{:S(2)}, u32[]{:S(2)}) collective-permute-start(bf16[64,7168]{1,0:T(8,128)(2,1)S(1)} %get-tuple-element.79), channel_id=1, source_target_pairs={{0,1},{1,0},{2,3},{3,2},{4,5},{5,4},{6,7},{7,6},{8,9},{9,8},{10,11... | collective-permute-start | bytes 2752520 | tf_op jit(solution)/shard_map/ppermute | solution.py:31
  53.9 29.1 %collective-permute-start.9 = (bf16[48,7168]{1,0:T(8,128)(2,1)S(1)}, bf16[48,7168]{1,0:T(8,128)(2,1)S(1)}, u32[]{:S(2)}, u32[]{:S(2)}) collective-permute-start(bf16[48,7168]{1,0:T(8,128)(2,1)S(1)} %get-tuple-element.58), channel_id=1, source_target_pairs={{0,2},{1,3},{2,4},{3,5},{4,6},{5,7},{6,0},{7,1},{8,10},{9,11},{10,... | collective-permute-start | bytes 2064392 | tf_op jit(solution)/shard_map/ppermute | solution.py:31
  53.9 32.8 %collective-permute-start.10 = (bf16[48,7168]{1,0:T(8,128)(2,1)S(1)}, bf16[48,7168]{1,0:T(8,128)(2,1)S(1)}, u32[]{:S(2)}, u32[]{:S(2)}) collective-permute-start(bf16[48,7168]{1,0:T(8,128)(2,1)S(1)} %get-tuple-element.59), channel_id=1, source_target_pairs={{0,6},{1,7},{2,0},{3,1},{4,2},{5,3},{6,4},{7,5},{8,14},{9,15},{10,... | collective-permute-start | bytes 2064392 | tf_op jit(solution)/shard_map/ppermute | solution.py:31
  72.0 7.7 %collective-permute-start.11 = (bf16[32,7168]{1,0:T(8,128)(2,1)S(1)}, bf16[32,7168]{1,0:T(8,128)(2,1)S(1)}, u32[]{:S(2)}, u32[]{:S(2)}) collective-permute-start(bf16[32,7168]{1,0:T(8,128)(2,1)S(1)} %pad_maximum_fusion.22), channel_id=1, source_target_pairs={{0,1},{1,0},{2,3},{3,2},{4,5},{5,4},{6,7},{7,6},{8,9},{9,8},{10,11... | collective-permute-start | bytes 1376264 | tf_op jit(solution)/shard_map/ppermute | solution.py:31
  73.5 24.3 %collective-permute-start.34 = (bf16[32,7168]{1,0:T(8,128)(2,1)S(1)}, bf16[32,7168]{1,0:T(8,128)(2,1)S(1)}, u32[]{:S(2)}, u32[]{:S(2)}) collective-permute-start(bf16[32,7168]{1,0:T(8,128)(2,1)S(1)} %pad_maximum_fusion.25), channel_id=1, source_target_pairs={{0,1},{1,0},{2,3},{3,2},{4,5},{5,4},{6,7},{7,6},{8,9},{9,8},{10,11... | collective-permute-start | bytes 1376264 | tf_op jit(solution)/shard_map/ppermute | solution.py:31
  79.7 7.1 %copy-start.21 = (bf16[32,7168]{1,0:T(8,128)(2,1)}, bf16[32,7168]{1,0:T(8,128)(2,1)S(1)}, u32[]{:S(2)}) copy-start(bf16[32,7168]{1,0:T(8,128)(2,1)S(1)} %collective-permute-done.11.refs_11_) | copy-start | bytes 1376260
  83.0 3.7 %copy-start.22 = (bf16[48,7168]{1,0:T(8,128)(2,1)}, bf16[48,7168]{1,0:T(8,128)(2,1)S(1)}, u32[]{:S(2)}) copy-start(bf16[48,7168]{1,0:T(8,128)(2,1)S(1)} %collective-permute-done.9.refs_6_) | copy-start | bytes 2064388
  86.8 11.2 %collective-permute-start.12 = (bf16[16,7168]{1,0:T(8,128)(2,1)S(1)}, bf16[16,7168]{1,0:T(8,128)(2,1)S(1)}, u32[]{:S(2)}, u32[]{:S(2)}) collective-permute-start(bf16[16,7168]{1,0:T(8,128)(2,1)S(1)} %slice.447), channel_id=1, source_target_pairs={{0,2},{1,3},{2,4},{3,5},{4,6},{5,7},{6,0},{7,1},{8,10},{9,11},{10,... | collective-permute-start | bytes 688136 | tf_op jit(solution)/shard_map/ppermute | solution.py:31
  87.6 13.3 %collective-permute-start.13 = (bf16[16,7168]{1,0:T(8,128)(2,1)S(1)}, bf16[16,7168]{1,0:T(8,128)(2,1)}, u32[]{:S(2)}, u32[]{:S(2)}) collective-permute-start(bf16[16,7168]{1,0:T(8,128)(2,1)S(1)} %slice.448), channel_id=1, source_target_pairs={{0,6},{1,7},{2,0},{3,1},{4,2},{5,3},{6,4},{7,5},{8,14},{9,15},{10,... | collective-permute-start | bytes 688136 | tf_op jit(solution)/shard_map/ppermute | solution.py:31
  90.2 33.6 %collective-permute-start.4 = (bf16[128,7168]{1,0:T(8,128)(2,1)}, bf16[128,7168]{1,0:T(8,128)(2,1)}, u32[]{:S(2)}, u32[]{:S(2)}) collective-permute-start(bf16[128,7168]{1,0:T(8,128)(2,1)} %bitcast.166), channel_id=1, source_target_pairs={{32,0},{33,1},{34,2},{35,3},{36,4},{37,5},{38,6},{39,7},{40,8},{41... | collective-permute-start | bytes 5505032 | tf_op jit(solution)/shard_map/ppermute | solution.py:38
  95.9 27.9 %collective-permute-start.5 = (f32[128,64]{1,0:T(8,128)S(1)}, f32[128,64]{1,0:T(8,128)S(1)}, u32[]{:S(2)}, u32[]{:S(2)}) collective-permute-start(f32[128,64]{1,0:T(8,128)S(1)} %and_select_fusion), channel_id=1, source_target_pairs={{32,0},{33,1},{34,2},{35,3},{36,4},{37,5},{38,6},{39,7},{40,8},{41... | collective-permute-start | bytes 98312 | tf_op jit(solution)/shard_map/ppermute | solution.py:38
  97.9 18.8 %copy-start.20 = (bf16[32,7168]{1,0:T(8,128)(2,1)}, bf16[32,7168]{1,0:T(8,128)(2,1)S(1)}, u32[]{:S(2)}) copy-start(bf16[32,7168]{1,0:T(8,128)(2,1)S(1)} %collective-permute-done.34.refs_11_) | copy-start | bytes 1376260
  97.9 21.2 %collective-permute-start.32 = (bf16[48,7168]{1,0:T(8,128)(2,1)S(1)}, bf16[48,7168]{1,0:T(8,128)(2,1)}, u32[]{:S(2)}, u32[]{:S(2)}) collective-permute-start(bf16[48,7168]{1,0:T(8,128)(2,1)S(1)} %get-tuple-element.80), channel_id=1, source_target_pairs={{0,2},{1,3},{2,4},{3,5},{4,6},{5,7},{6,0},{7,1},{8,10},{9,11},{10,... | collective-permute-start | bytes 2064392 | tf_op jit(solution)/shard_map/ppermute | solution.py:31
  98.0 2.9 %copy-start.28 = (bf16[16,7168]{1,0:T(8,128)(2,1)}, bf16[16,7168]{1,0:T(8,128)(2,1)S(1)}, u32[]{:S(2)}) copy-start(bf16[16,7168]{1,0:T(8,128)(2,1)S(1)} %collective-permute-done.12.refs_10_) | copy-start | bytes 688132
  98.0 22.0 %collective-permute-start.33 = (bf16[48,7168]{1,0:T(8,128)(2,1)S(1)}, bf16[48,7168]{1,0:T(8,128)(2,1)}, u32[]{:S(2)}, u32[]{:S(2)}) collective-permute-start(bf16[48,7168]{1,0:T(8,128)(2,1)S(1)} %get-tuple-element.81), channel_id=1, source_target_pairs={{0,6},{1,7},{2,0},{3,1},{4,2},{5,3},{6,4},{7,5},{8,14},{9,15},{10,... | collective-permute-start | bytes 2064392 | tf_op jit(solution)/shard_map/ppermute | solution.py:31
  120.1 8.8 %collective-permute-start.35 = (bf16[16,7168]{1,0:T(8,128)(2,1)S(1)}, bf16[16,7168]{1,0:T(8,128)(2,1)S(1)}, u32[]{:S(2)}, u32[]{:S(2)}) collective-permute-start(bf16[16,7168]{1,0:T(8,128)(2,1)S(1)} %slice.499), channel_id=1, source_target_pairs={{0,2},{1,3},{2,4},{3,5},{4,6},{5,7},{6,0},{7,1},{8,10},{9,11},{10,... | collective-permute-start | bytes 688136 | tf_op jit(solution)/shard_map/ppermute | solution.py:31
  120.1 9.4 %collective-permute-start.36 = (bf16[16,7168]{1,0:T(8,128)(2,1)S(1)}, bf16[16,7168]{1,0:T(8,128)(2,1)}, u32[]{:S(2)}, u32[]{:S(2)}) collective-permute-start(bf16[16,7168]{1,0:T(8,128)(2,1)S(1)} %slice.500), channel_id=1, source_target_pairs={{0,6},{1,7},{2,0},{3,1},{4,2},{5,3},{6,4},{7,5},{8,14},{9,15},{10,... | collective-permute-start | bytes 688136 | tf_op jit(solution)/shard_map/ppermute | solution.py:31
  123.8 21.5 %copy-start.14 = (f32[128,64]{1,0:T(8,128)}, f32[128,64]{1,0:T(8,128)S(1)}, u32[]{:S(2)}) copy-start(f32[128,64]{1,0:T(8,128)S(1)} %collective-permute-done.5) | copy-start | bytes 98308
  123.8 26.3 %collective-permute-start.15 = (bf16[64,7296]{1,0:T(8,128)(2,1)}, bf16[64,7296]{1,0:T(8,128)(2,1)S(1)}, u32[]{:S(2)}, u32[]{:S(2)}) collective-permute-start(bf16[64,7296]{1,0:T(8,128)(2,1)} %pad_maximum_fusion.8), channel_id=1, source_target_pairs={{0,1},{1,0},{2,3},{3,2},{4,5},{5,4},{6,7},{7,6},{8,9},{9,8},{10,11... | collective-permute-start | bytes 2801672 | tf_op jit(solution)/shard_map/ppermute | solution.py:31
  123.9 23.5 %collective-permute-start.14 = (bf16[16,7296]{1,0:T(8,128)(2,1)}, bf16[16,7296]{1,0:T(8,128)(2,1)}, u32[]{:S(2)}, u32[]{:S(2)}) collective-permute-start(bf16[16,7296]{1,0:T(8,128)(2,1)} %get-tuple-element.63), channel_id=1, source_target_pairs={{0,2},{1,3},{2,4},{3,5},{4,6},{5,7},{6,0},{7,1},{8,10},{9,11},{10,... | collective-permute-start | bytes 700424 | tf_op jit(solution)/shard_map/ppermute | solution.py:31
  124.0 26.1 %collective-permute-start.16 = (bf16[16,7296]{1,0:T(8,128)(2,1)S(1)}, bf16[16,7296]{1,0:T(8,128)(2,1)}, u32[]{:S(2)}, u32[]{:S(2)}) collective-permute-start(bf16[16,7296]{1,0:T(8,128)(2,1)S(1)} %get-tuple-element.65), channel_id=1, source_target_pairs={{0,6},{1,7},{2,0},{3,1},{4,2},{5,3},{6,4},{7,5},{8,14},{9,15},{10,... | collective-permute-start | bytes 700424 | tf_op jit(solution)/shard_map/ppermute | solution.py:31
  145.3 4.8 %copy-start.2 = (bf16[256,7296]{1,0:T(8,128)(2,1)S(1)}, bf16[256,7296]{1,0:T(8,128)(2,1)}, u32[]{:S(2)}) copy-start(bf16[256,7296]{1,0:T(8,128)(2,1)} %shard_map.95) | copy-start | bytes 11206660
  147.2 22.4 %collective-permute-start.38 = (bf16[64,7296]{1,0:T(8,128)(2,1)S(1)}, bf16[64,7296]{1,0:T(8,128)(2,1)S(1)}, u32[]{:S(2)}, u32[]{:S(2)}) collective-permute-start(bf16[64,7296]{1,0:T(8,128)(2,1)S(1)} %pad_maximum_fusion.9), channel_id=1, source_target_pairs={{0,1},{1,0},{2,3},{3,2},{4,5},{5,4},{6,7},{7,6},{8,9},{9,8},{10,11... | collective-permute-start | bytes 2801672 | tf_op jit(solution)/shard_map/ppermute | solution.py:31
  147.3 8.3 %collective-permute-start.37 = (bf16[16,7296]{1,0:T(8,128)(2,1)S(1)}, bf16[16,7296]{1,0:T(8,128)(2,1)S(1)}, u32[]{:S(2)}, u32[]{:S(2)}) collective-permute-start(bf16[16,7296]{1,0:T(8,128)(2,1)S(1)} %get-tuple-element.85), channel_id=1, source_target_pairs={{0,2},{1,3},{2,4},{3,5},{4,6},{5,7},{6,0},{7,1},{8,10},{9,11},{10,... | collective-permute-start | bytes 700424 | tf_op jit(solution)/shard_map/ppermute | solution.py:31
  147.4 8.2 %collective-permute-start.39 = (bf16[16,7296]{1,0:T(8,128)(2,1)S(1)}, bf16[16,7296]{1,0:T(8,128)(2,1)S(1)}, u32[]{:S(2)}, u32[]{:S(2)}) collective-permute-start(bf16[16,7296]{1,0:T(8,128)(2,1)S(1)} %get-tuple-element.87), channel_id=1, source_target_pairs={{0,6},{1,7},{2,0},{3,1},{4,2},{5,3},{6,4},{7,5},{8,14},{9,15},{10,... | collective-permute-start | bytes 700424 | tf_op jit(solution)/shard_map/ppermute | solution.py:31
  150.1 19.5 %copy-start.3 = (bf16[256,7296]{1,0:T(8,128)(2,1)S(1)}, bf16[256,7296]{1,0:T(8,128)(2,1)}, u32[]{:S(2)}) copy-start(bf16[256,7296]{1,0:T(8,128)(2,1)} %shard_map.97) | copy-start | bytes 11206660
  151.7 20.0 %collective-permute-start.18 = (bf16[40,7296]{1,0:T(8,128)(2,1)S(1)}, bf16[40,7296]{1,0:T(8,128)(2,1)S(1)}, u32[]{:S(2)}, u32[]{:S(2)}) collective-permute-start(bf16[40,7296]{1,0:T(8,128)(2,1)S(1)} %pad_maximum_fusion.17), channel_id=1, source_target_pairs={{0,6},{1,7},{2,0},{3,1},{4,2},{5,3},{6,4},{7,5},{8,14},{9,15},{10,... | collective-permute-start | bytes 1751048 | tf_op jit(solution)/shard_map/ppermute | solution.py:31
  152.7 19.1 %collective-permute-start.17 = (bf16[40,7296]{1,0:T(8,128)(2,1)S(1)}, bf16[40,7296]{1,0:T(8,128)(2,1)S(1)}, u32[]{:S(2)}, u32[]{:S(2)}) collective-permute-start(bf16[40,7296]{1,0:T(8,128)(2,1)S(1)} %pad_maximum_fusion.16), channel_id=1, source_target_pairs={{0,2},{1,3},{2,4},{3,5},{4,6},{5,7},{6,0},{7,1},{8,10},{9,11},{10,... | collective-permute-start | bytes 1751048 | tf_op jit(solution)/shard_map/ppermute | solution.py:31
  170.0 14.0 %collective-permute-start.41 = (bf16[40,7296]{1,0:T(8,128)(2,1)S(1)}, bf16[40,7296]{1,0:T(8,128)(2,1)S(1)}, u32[]{:S(2)}, u32[]{:S(2)}) collective-permute-start(bf16[40,7296]{1,0:T(8,128)(2,1)S(1)} %pad_maximum_fusion.19), channel_id=1, source_target_pairs={{0,6},{1,7},{2,0},{3,1},{4,2},{5,3},{6,4},{7,5},{8,14},{9,15},{10,... | collective-permute-start | bytes 1751048 | tf_op jit(solution)/shard_map/ppermute | solution.py:31
  171.7 14.3 %collective-permute-start.40 = (bf16[40,7296]{1,0:T(8,128)(2,1)S(1)}, bf16[40,7296]{1,0:T(8,128)(2,1)S(1)}, u32[]{:S(2)}, u32[]{:S(2)}) collective-permute-start(bf16[40,7296]{1,0:T(8,128)(2,1)S(1)} %pad_maximum_fusion.18), channel_id=1, source_target_pairs={{0,2},{1,3},{2,4},{3,5},{4,6},{5,7},{6,0},{7,1},{8,10},{9,11},{10,... | collective-permute-start | bytes 1751048 | tf_op jit(solution)/shard_map/ppermute | solution.py:31
  172.0 14.4 %collective-permute-start.19 = (bf16[16,7296]{1,0:T(8,128)(2,1)S(1)}, bf16[16,7296]{1,0:T(8,128)(2,1)S(1)}, u32[]{:S(2)}, u32[]{:S(2)}) collective-permute-start(bf16[16,7296]{1,0:T(8,128)(2,1)S(1)} %fusion.23), channel_id=1, source_target_pairs={{0,1},{1,0},{2,3},{3,2},{4,5},{5,4},{6,7},{7,6},{8,9},{9,8},{10,11... | collective-permute-start | bytes 700424 | tf_op jit(solution)/shard_map/ppermute | solution.py:31
  172.2 18.8 %collective-permute-start.20 = (bf16[16,7296]{1,0:T(8,128)(2,1)S(1)}, bf16[16,7296]{1,0:T(8,128)(2,1)S(1)}, u32[]{:S(2)}, u32[]{:S(2)}) collective-permute-start(bf16[16,7296]{1,0:T(8,128)(2,1)S(1)} %pad_maximum_fusion.26), channel_id=1, source_target_pairs={{0,2},{1,3},{2,4},{3,5},{4,6},{5,7},{6,0},{7,1},{8,10},{9,11},{10,... | collective-permute-start | bytes 700424 | tf_op jit(solution)/shard_map/ppermute | solution.py:31
  172.2 18.8 %collective-permute-start.21 = (bf16[16,7296]{1,0:T(8,128)(2,1)S(1)}, bf16[16,7296]{1,0:T(8,128)(2,1)S(1)}, u32[]{:S(2)}, u32[]{:S(2)}) collective-permute-start(bf16[16,7296]{1,0:T(8,128)(2,1)S(1)} %pad_maximum_fusion.27), channel_id=1, source_target_pairs={{0,6},{1,7},{2,0},{3,1},{4,2},{5,3},{6,4},{7,5},{8,14},{9,15},{10,... | collective-permute-start | bytes 700424 | tf_op jit(solution)/shard_map/ppermute | solution.py:31
  186.2 12.9 %collective-permute-start.42 = (bf16[16,7296]{1,0:T(8,128)(2,1)S(1)}, bf16[16,7296]{1,0:T(8,128)(2,1)S(1)}, u32[]{:S(2)}, u32[]{:S(2)}) collective-permute-start(bf16[16,7296]{1,0:T(8,128)(2,1)S(1)} %fusion.12), channel_id=1, source_target_pairs={{0,1},{1,0},{2,3},{3,2},{4,5},{5,4},{6,7},{7,6},{8,9},{9,8},{10,11... | collective-permute-start | bytes 700424 | tf_op jit(solution)/shard_map/ppermute | solution.py:31
  186.4 14.7 %collective-permute-start.43 = (bf16[16,7296]{1,0:T(8,128)(2,1)S(1)}, bf16[16,7296]{1,0:T(8,128)(2,1)S(1)}, u32[]{:S(2)}, u32[]{:S(2)}) collective-permute-start(bf16[16,7296]{1,0:T(8,128)(2,1)S(1)} %pad_maximum_fusion.28), channel_id=1, source_target_pairs={{0,2},{1,3},{2,4},{3,5},{4,6},{5,7},{6,0},{7,1},{8,10},{9,11},{10,... | collective-permute-start | bytes 700424 | tf_op jit(solution)/shard_map/ppermute | solution.py:31
  186.4 14.7 %collective-permute-start.44 = (bf16[16,7296]{1,0:T(8,128)(2,1)S(1)}, bf16[16,7296]{1,0:T(8,128)(2,1)S(1)}, u32[]{:S(2)}, u32[]{:S(2)}) collective-permute-start(bf16[16,7296]{1,0:T(8,128)(2,1)S(1)} %pad_maximum_fusion.29), channel_id=1, source_target_pairs={{0,6},{1,7},{2,0},{3,1},{4,2},{5,3},{6,4},{7,5},{8,14},{9,15},{10,... | collective-permute-start | bytes 700424 | tf_op jit(solution)/shard_map/ppermute | solution.py:31
  191.3 28.6 %collective-permute-start.47 = (bf16[16,128]{1,0:T(8,128)(2,1)S(1)}, bf16[16,128]{1,0:T(8,128)(2,1)S(1)}, u32[]{:S(2)}, u32[]{:S(2)}) collective-permute-start(bf16[16,128]{1,0:T(8,128)(2,1)S(1)} %slice.482), channel_id=1, source_target_pairs={{0,24},{1,25},{2,26},{3,27},{4,28},{5,29},{6,30},{7,31},{8,0},{9,1... | collective-permute-start | bytes 12296 | tf_op jit(solution)/shard_map/ppermute | solution.py:31
  192.1 12.9 %collective-permute-start.22 = (bf16[16,7168]{1,0:T(8,128)(2,1)S(1)}, bf16[16,7168]{1,0:T(8,128)(2,1)S(1)}, u32[]{:S(2)}, u32[]{:S(2)}) collective-permute-start(bf16[16,7168]{1,0:T(8,128)(2,1)S(1)} %slice.479), channel_id=1, source_target_pairs={{32,0},{33,1},{34,2},{35,3},{36,4},{37,5},{38,6},{39,7},{40,8},{41... | collective-permute-start | bytes 688136 | tf_op jit(solution)/shard_map/ppermute | solution.py:38
  199.1 11.2 %collective-permute-start.23 = (bf16[16,7168]{1,0:T(8,128)(2,1)S(1)}, bf16[16,7168]{1,0:T(8,128)(2,1)S(1)}, u32[]{:S(2)}, u32[]{:S(2)}) collective-permute-start(bf16[16,7168]{1,0:T(8,128)(2,1)S(1)} %slice.483), channel_id=1, source_target_pairs={{32,24},{33,25},{34,26},{35,27},{36,28},{37,29},{38,30},{39,31},{4... | collective-permute-start | bytes 688136 | tf_op jit(solution)/shard_map/ppermute | solution.py:38
  201.4 18.6 %collective-permute-start.48 = (bf16[16,128]{1,0:T(8,128)(2,1)S(1)}, bf16[16,128]{1,0:T(8,128)(2,1)S(1)}, u32[]{:S(2)}, u32[]{:S(2)}) collective-permute-start(bf16[16,128]{1,0:T(8,128)(2,1)S(1)} %slice.535), channel_id=1, source_target_pairs={{0,16},{1,17},{2,18},{3,19},{4,20},{5,21},{6,22},{7,23},{8,24},{9,... | collective-permute-start | bytes 12296 | tf_op jit(solution)/shard_map/ppermute | solution.py:31
  203.2 16.8 %collective-permute-start.49 = (bf16[16,128]{1,0:T(8,128)(2,1)S(1)}, bf16[16,128]{1,0:T(8,128)(2,1)S(1)}, u32[]{:S(2)}, u32[]{:S(2)}) collective-permute-start(bf16[16,128]{1,0:T(8,128)(2,1)S(1)} %slice.531), channel_id=1, source_target_pairs={{0,8},{1,9},{2,10},{3,11},{4,12},{5,13},{6,14},{7,15},{8,16},{9,17... | collective-permute-start | bytes 12296 | tf_op jit(solution)/shard_map/ppermute | solution.py:31
  205.0 5.3 %copy-start.29 = (bf16[16,7168]{1,0:T(8,128)(2,1)}, bf16[16,7168]{1,0:T(8,128)(2,1)S(1)}, u32[]{:S(2)}) copy-start(bf16[16,7168]{1,0:T(8,128)(2,1)S(1)} %collective-permute-done.22.refs_0_) | copy-start | bytes 688132
  205.0 15.8 %collective-permute-start.45 = (bf16[16,7168]{1,0:T(8,128)(2,1)S(1)}, bf16[16,7168]{1,0:T(8,128)(2,1)S(1)}, u32[]{:S(2)}, u32[]{:S(2)}) collective-permute-start(bf16[16,7168]{1,0:T(8,128)(2,1)S(1)} %slice.536), channel_id=1, source_target_pairs={{32,16},{33,17},{34,18},{35,19},{36,20},{37,21},{38,22},{39,23},{4... | collective-permute-start | bytes 688136 | tf_op jit(solution)/shard_map/ppermute | solution.py:38
  211.0 18.0 %copy-start.15 = (f32[128,64]{1,0:T(8,128)S(1)}, f32[128,64]{1,0:T(8,128)}, u32[]{:S(2)}) copy-start(f32[128,64]{1,0:T(8,128)} %copy-done.14) | copy-start | bytes 98308
  218.0 10.9 %collective-permute-start.46 = (bf16[16,7168]{1,0:T(8,128)(2,1)S(1)}, bf16[16,7168]{1,0:T(8,128)(2,1)S(1)}, u32[]{:S(2)}, u32[]{:S(2)}) collective-permute-start(bf16[16,7168]{1,0:T(8,128)(2,1)S(1)} %slice.532), channel_id=1, source_target_pairs={{32,8},{33,9},{34,10},{35,11},{36,12},{37,13},{38,14},{39,15},{40,... | collective-permute-start | bytes 688136 | tf_op jit(solution)/shard_map/ppermute | solution.py:38
  (18 other events, 24.2 us)
where the time goes:
time: 235 us; the launch traced here: 234 us
  waiting for transfers between devices  97.1 us (41%)
  starting transfers between devices  68.8 us (29%)
  Pallas kernels  38.5 us (16%)
  local copies, waits for them, and re-layouts  17.2 us (7%)
  other arithmetic  8.76 us (4%)
    ppermute x44, waiting for transfers between devices, send(): return lax.ppermute(block, 'expert', route)  83.7 us
    ppermute x44, starting transfers between devices, send(): return lax.ppermute(block, 'expert', route)  48.5 us
    pallas_call x2, Pallas kernels, experts_backward(): pl.pallas_call(kernel, out_shape=jax.ShapeDtypeStruct((rows, depth + MARK...  31.5 us
    ppermute x6, starting transfers between devices, send(): return lax.ppermute(block, ('pipe', 'expert'), route)  20.3 us
    ppermute x6, waiting for transfers between devices, send(): return lax.ppermute(block, ('pipe', 'expert'), route)  13.4 us
    unnamed x65, local copies, waits for them, and re-layouts  8.89 us
    pallas_call x1, Pallas kernels, blend(): pl.pallas_call(kernel, grid=(width // step,), out_shape=jax.ShapeDtypeStr...  7.01 us
  transfers between devices with their start and end apart: 50, of which 18 were waited for; matrix products, arithmetic and copies ran while one was open for 6% of the time, Pallas kernels for 16%

commit v1 on v0

--- a/solution.py
+++ b/solution.py
@@ -8,8 +8,8 @@
 CAP = 16
 MARKS = 128
 NX, NY, NZ = 4, 4, 2
-TIED = ()
 FLOPS = 40
+HOME = 7
 BLEND = 25000000000
 VMEM = pl.BlockSpec(memory_space=pltpu.VMEM)
 SMEM = pl.BlockSpec(memory_space=pltpu.SMEM)
@@ -387,7 +387,7 @@
         yield links
         two.third(links)
         yield links
-        sums = compute(dxs, [LateCross, SoonCross])
+        sums = compute(dxs, [SoonCross, LateCross] if 0 in dxs else [SoonCross, LateCross])
         for part in sums:
             part.first(links)
         yield links
@@ -403,17 +403,21 @@
 
     for phase, (early, late) in enumerate(zip(chain((0, 1)), chain((3, 2)))):
         early.run()
-        late.run(early.last if phase in TIED else ())
-
-    mix = value(back["mixing"])
-    early = blend(value(back["grads"]), mix[:, : 2 * CAP], [value(moved[dx]) for dx in (0, 1)])
+        others = ()
+        if phase == HOME:
+            mix = value(back["mixing"])
+            near = [value(moved[dx]) for dx in (0, 1)]
+            mixed = blend(value(back["grads"]), mix[:, : 2 * CAP], near)
+            others = [mixed]
+        late.run(others)
+
     sums = jnp.concatenate([value(moved[dx]) for dx in (2, 3)])
     mix = mix[:, 2 * CAP :]
     high = lax.reduce_precision(mix, 8, 7)
     moe_grad = jnp.dot(
         high.astype(jnp.bfloat16), sums, preferred_element_type=jnp.float32
     ) + jnp.dot((mix - high).astype(jnp.bfloat16), sums, preferred_element_type=jnp.float32)
-    passed = (early + moe_grad).astype(jnp.bfloat16)
+    passed = (mixed + moe_grad).astype(jnp.bfloat16)
     last_section = lax.axis_index("pipe") == lax.axis_size("pipe") - 1
     next_grad = jnp.where(last_section, head_grad, passed)
 

time: 235 us -> 233 us (level)
  waiting for transfers between devices: 97.1 us -> 85.8 us
  starting transfers between devices: 68.8 us -> 73.5 us
  other arithmetic: 8.76 us -> 12.2 us
    ppermute x44, waiting for transfers between devices: 83.7 us -> 73 us  [send(): return lax.ppermute(block, 'expert', route)]
    ppermute x44, starting transfers between devices: 48.5 us -> 53 us  [send(): return lax.ppermute(block, 'expert', route)]
    convert_element_type x10, other arithmetic: 2.58 us -> 7.07 us  [added(): return total.astype(jnp.bfloat16)]
  transfers between devices with their start and end apart: 50 -> 50, of which waited for: 18 -> 19; matrix products, arithmetic and copies ran while one was open for 6% -> 8% of each run, Pallas kernels for 16% -> 17%
where the time goes in v1:
time: 233 us; the launch traced here: 232 us
  waiting for transfers between devices  85.8 us (37%)
  starting transfers between devices  73.5 us (32%)
  Pallas kernels  38.5 us (17%)
  local copies, waits for them, and re-layouts  17.2 us (7%)
  other arithmetic  12.2 us (5%)
  matrix products  3.52 us (2%)
    ppermute x44, waiting for transfers between devices, send(): return lax.ppermute(block, 'expert', route)  73 us
    ppermute x44, starting transfers between devices, send(): return lax.ppermute(block, 'expert', route)  53 us
    pallas_call x2, Pallas kernels, experts_backward(): pl.pallas_call(kernel, out_shape=jax.ShapeDtypeStruct((rows, depth + MARK...  31.5 us
    ppermute x6, starting transfers between devices, send(): return lax.ppermute(block, ('pipe', 'expert'), route)  20.5 us
    ppermute x6, waiting for transfers between devices, send(): return lax.ppermute(block, ('pipe', 'expert'), route)  12.8 us
    unnamed x65, local copies, waits for them, and re-layouts  8.86 us
    convert_element_type x10, other arithmetic, added(): return total.astype(jnp.bfloat16)  7.07 us
    pallas_call x1, Pallas kernels, blend(): pl.pallas_call(kernel, grid=(width // step,), out_shape=jax.ShapeDtypeStr...  6.98 us
  transfers between devices with their start and end apart: 50, of which 19 were waited for; matrix products, arithmetic and copies ran while one was open for 8% of the time, Pallas kernels for 17%

profile of v1, /device:TPU:1, one launch (start us, length us, event | category | flops | bytes accessed | tf_op | source)
XLA Modules:
  0.0 232.4 jit_solution(4786073474855842709)
XLA Ops:
  0.7 0.9 compare_reduce_fusion
  2.6 1.0 copy-done.4
  4.2 3.4 %collective-permute-start.24 = (bf16[32,7168]{1,0:T(8,128)(2,1)S(1)}, bf16[32,7168]{1,0:T(8,128)(2,1)S(1)}, u32[]{:S(2)}, u32[]{:S(2)}) collective-permute-start(bf16[32,7168]{1,0:T(8,128)(2,1)S(1)} %pad_maximum_fusion.23), channel_id=1, source_target_pairs={{0,24},{1,25},{2,26},{3,27},{4,28},{5,29},{6,30},{7,31},{8,0},{9,1... | collective-permute-start | bytes 1376264 | tf_op jit(solution)/shard_map/ppermute | solution.py:31
  7.6 1.4 collective-permute-start.1
  9.0 1.6 collective-permute-start.2
  10.6 1.5 collective-permute-start.3
  12.9 3.9 %collective-permute-done.24.refs_0_ = bf16[32,7168]{1,0:T(8,128)(2,1)S(1)} collective-permute-done((bf16[32,7168]{1,0:T(8,128)(2,1)S(1)}, bf16[32,7168]{1,0:T(8,128)(2,1)S(1)}, u32[]{:S(2)}, u32[]{:S(2)}) %collective-permute-start.24) | collective-permute-done | bytes 458784 | tf_op jit(solution)/shard_map/ppermute | solution.py:31
  16.8 1.3 collective-permute-start.27
  18.0 2.1 collective-permute-done.1.refs_3_
  20.1 1.7 collective-permute-start.28
  21.8 1.6 collective-permute-start.25
  23.4 1.0 slice.437
  25.0 1.0 slice.438
  26.7 3.4 %collective-permute-done.27.refs_3_ = bf16[32,7168]{1,0:T(8,128)(2,1)S(1)} collective-permute-done((bf16[32,7168]{1,0:T(8,128)(2,1)S(1)}, bf16[32,7168]{1,0:T(8,128)(2,1)S(1)}, u32[]{:S(2)}, u32[]{:S(2)}) %collective-permute-start.27) | collective-permute-done | bytes 458784 | tf_op jit(solution)/shard_map/ppermute | solution.py:31
  30.1 1.4 collective-permute-start.7
  31.6 1.7 collective-permute-start.8
  33.4 1.5 collective-permute-done.26.refs_7_
  35.7 2.7 %collective-permute-start.30 = (bf16[64,7168]{1,0:T(8,128)(2,1)S(1)}, bf16[64,7168]{1,0:T(8,128)(2,1)S(1)}, u32[]{:S(2)}, u32[]{:S(2)}) collective-permute-start(bf16[64,7168]{1,0:T(8,128)(2,1)S(1)} %get-tuple-element.78), channel_id=1, source_target_pairs={{0,6},{1,7},{2,0},{3,1},{4,2},{5,3},{6,4},{7,5},{8,14},{9,15},{10,... | collective-permute-start | bytes 2752520 | tf_op jit(solution)/shard_map/ppermute | solution.py:31
  38.4 14.2 %collective-permute-done.7.refs_5_ = bf16[64,7168]{1,0:T(8,128)(2,1)S(1)} collective-permute-done((bf16[64,7168]{1,0:T(8,128)(2,1)S(1)}, bf16[64,7168]{1,0:T(8,128)(2,1)S(1)}, u32[]{:S(2)}, u32[]{:S(2)}) %collective-permute-start.7) | collective-permute-done | bytes 917536 | tf_op jit(solution)/shard_map/ppermute | solution.py:31
  54.1 2.7 %collective-permute-start.10 = (bf16[48,7168]{1,0:T(8,128)(2,1)S(1)}, bf16[48,7168]{1,0:T(8,128)(2,1)S(1)}, u32[]{:S(2)}, u32[]{:S(2)}) collective-permute-start(bf16[48,7168]{1,0:T(8,128)(2,1)S(1)} %get-tuple-element.59), channel_id=1, source_target_pairs={{0,6},{1,7},{2,0},{3,1},{4,2},{5,3},{6,4},{7,5},{8,14},{9,15},{10,... | collective-permute-start | bytes 2064392 | tf_op jit(solution)/shard_map/ppermute | solution.py:31
  56.8 15.4 %collective-permute-done.30.refs_5_ = bf16[64,7168]{1,0:T(8,128)(2,1)S(1)} collective-permute-done((bf16[64,7168]{1,0:T(8,128)(2,1)S(1)}, bf16[64,7168]{1,0:T(8,128)(2,1)S(1)}, u32[]{:S(2)}, u32[]{:S(2)}) %collective-permute-start.30) | collective-permute-done | bytes 917536 | tf_op jit(solution)/shard_map/ppermute | solution.py:31
  73.7 1.2 collective-permute-start.34
  75.0 5.7 %collective-permute-done.11.refs_11_ = bf16[32,7168]{1,0:T(8,128)(2,1)S(1)} collective-permute-done((bf16[32,7168]{1,0:T(8,128)(2,1)S(1)}, bf16[32,7168]{1,0:T(8,128)(2,1)S(1)}, u32[]{:S(2)}, u32[]{:S(2)}) %collective-permute-start.11) | collective-permute-done | bytes 458784 | tf_op jit(solution)/shard_map/ppermute | solution.py:31
  80.6 2.4 %collective-permute-done.9.refs_6_ = bf16[48,7168]{1,0:T(8,128)(2,1)S(1)} collective-permute-done((bf16[48,7168]{1,0:T(8,128)(2,1)S(1)}, bf16[48,7168]{1,0:T(8,128)(2,1)S(1)}, u32[]{:S(2)}, u32[]{:S(2)}) %collective-permute-start.9) | collective-permute-done | bytes 688160 | tf_op jit(solution)/shard_map/ppermute | solution.py:31
  83.0 3.9 %collective-permute-done.10.refs_9_ = bf16[48,7168]{1,0:T(8,128)(2,1)S(1)} collective-permute-done((bf16[48,7168]{1,0:T(8,128)(2,1)S(1)}, bf16[48,7168]{1,0:T(8,128)(2,1)S(1)}, u32[]{:S(2)}, u32[]{:S(2)}) %collective-permute-start.10) | collective-permute-done | bytes 688160 | tf_op jit(solution)/shard_map/ppermute | solution.py:31
  87.8 2.4 %collective-permute-start.13 = (bf16[16,7168]{1,0:T(8,128)(2,1)S(1)}, bf16[16,7168]{1,0:T(8,128)(2,1)}, u32[]{:S(2)}, u32[]{:S(2)}) collective-permute-start(bf16[16,7168]{1,0:T(8,128)(2,1)S(1)} %slice.448), channel_id=1, source_target_pairs={{0,6},{1,7},{2,0},{3,1},{4,2},{5,3},{6,4},{7,5},{8,14},{9,15},{10,... | collective-permute-start | bytes 688136 | tf_op jit(solution)/shard_map/ppermute | solution.py:31
  90.2 5.3 %collective-permute-start.4 = (bf16[128,7168]{1,0:T(8,128)(2,1)}, bf16[128,7168]{1,0:T(8,128)(2,1)}, u32[]{:S(2)}, u32[]{:S(2)}) collective-permute-start(bf16[128,7168]{1,0:T(8,128)(2,1)} %bitcast.166), channel_id=1, source_target_pairs={{32,0},{33,1},{34,2},{35,3},{36,4},{37,5},{38,6},{39,7},{40,8},{41... | collective-permute-start | bytes 5505032 | tf_op jit(solution)/shard_map/ppermute | solution.py:38
  95.5 1.9 collective-permute-start.5
  97.6 2.9 %collective-permute-start.33 = (bf16[48,7168]{1,0:T(8,128)(2,1)S(1)}, bf16[48,7168]{1,0:T(8,128)(2,1)}, u32[]{:S(2)}, u32[]{:S(2)}) collective-permute-start(bf16[48,7168]{1,0:T(8,128)(2,1)S(1)} %get-tuple-element.81), channel_id=1, source_target_pairs={{0,6},{1,7},{2,0},{3,1},{4,2},{5,3},{6,4},{7,5},{8,14},{9,15},{10,... | collective-permute-start | bytes 2064392 | tf_op jit(solution)/shard_map/ppermute | solution.py:31
  100.5 15.8 %shard_map.95 = bf16[256,7296]{1,0:T(8,128)(2,1)} custom-call(s32[1]{0:T(128)} %bitcast.13.piece_ref, bf16[32,7168]{1,0:T(8,128)(2,1)} %copy-done.8, bf16[32,7168]{1,0:T(8,128)(2,1)} %collective-permute-done.3.refs_1_, bf16[64,7168]{1,0:T(8,128)(2,1)} %copy-done.7, bf16[32,7168]{1,0:T(8,128)(2,1)} %copy-done.10, ...), custom_call_target="tpu_custom_call" | custom-call | flops 18790481920 | bytes 22020096 | tf_op jit(solution)/shard_map/pallas_call | solution.py:270
  116.3 2.5 %slice_bitcast_fusion.20 = (bf16[16,7296]{1,0:T(8,128)(2,1)S(1)}, bf16[16,7296]{1,0:T(8,128)(2,1)S(1)}, bf16[16,7296]{1,0:T(8,128)(2,1)}, bf16[16,7296]{1,0:T(8,...) fusion(bf16[2,8,16,7296]{3,2,1,0:T(8,128)(2,1)} %bitcast.162), kind=kLoop, calls=%fused_computation.99 | loop fusion | bytes 3735552 | tf_op jit(solution)/shard_map/squeeze | solution.py:360
  118.8 1.0 slice.499
  119.8 2.7 %collective-permute-start.36 = (bf16[16,7168]{1,0:T(8,128)(2,1)S(1)}, bf16[16,7168]{1,0:T(8,128)(2,1)S(1)}, u32[]{:S(2)}, u32[]{:S(2)}) collective-permute-start(bf16[16,7168]{1,0:T(8,128)(2,1)S(1)} %slice.500), channel_id=1, source_target_pairs={{0,6},{1,7},{2,0},{3,1},{4,2},{5,3},{6,4},{7,5},{8,14},{9,15},{10,... | collective-permute-start | bytes 688136 | tf_op jit(solution)/shard_map/ppermute | solution.py:31
  122.5 1.0 pad_maximum_fusion.8
  124.0 2.7 %collective-permute-start.16 = (bf16[16,7296]{1,0:T(8,128)(2,1)}, bf16[16,7296]{1,0:T(8,128)(2,1)S(1)}, u32[]{:S(2)}, u32[]{:S(2)}) collective-permute-start(bf16[16,7296]{1,0:T(8,128)(2,1)} %get-tuple-element.65), channel_id=1, source_target_pairs={{0,6},{1,7},{2,0},{3,1},{4,2},{5,3},{6,4},{7,5},{8,14},{9,15},{10,... | collective-permute-start | bytes 700424 | tf_op jit(solution)/shard_map/ppermute | solution.py:31
  126.6 1.5 collective-permute-done.35.refs_10_
  129.5 15.7 %shard_map.97 = bf16[256,7296]{1,0:T(8,128)(2,1)} custom-call(s32[1]{0:T(128)} %bitcast.13.piece_ref, bf16[32,7168]{1,0:T(8,128)(2,1)} %copy-done.27, bf16[32,7168]{1,0:T(8,128)(2,1)} %copy-done.18, bf16[64,7168]{1,0:T(8,128)(2,1)} %copy-done.6, bf16[32,7168]{1,0:T(8,128)(2,1)} %copy-done.9, bf16[32,7168]{1,0:T(8,128)(2,1)} %copy-done.17, ...), custom_call_target="tpu_custom_call" | custom-call | flops 18790481920 | bytes 22020096 | tf_op jit(solution)/shard_map/pallas_call | solution.py:270
  145.3 1.8 slice_bitcast_fusion.4
  147.6 2.7 %collective-permute-start.39 = (bf16[16,7296]{1,0:T(8,128)(2,1)S(1)}, bf16[16,7296]{1,0:T(8,128)(2,1)S(1)}, u32[]{:S(2)}, u32[]{:S(2)}) collective-permute-start(bf16[16,7296]{1,0:T(8,128)(2,1)S(1)} %get-tuple-element.87), channel_id=1, source_target_pairs={{0,6},{1,7},{2,0},{3,1},{4,2},{5,3},{6,4},{7,5},{8,14},{9,15},{10,... | collective-permute-start | bytes 700424 | tf_op jit(solution)/shard_map/ppermute | solution.py:31
  150.3 1.5 fusion.26
  152.0 2.7 %collective-permute-start.18 = (bf16[40,7296]{1,0:T(8,128)(2,1)S(1)}, bf16[40,7296]{1,0:T(8,128)(2,1)S(1)}, u32[]{:S(2)}, u32[]{:S(2)}) collective-permute-start(bf16[40,7296]{1,0:T(8,128)(2,1)S(1)} %pad_maximum_fusion.17), channel_id=1, source_target_pairs={{0,6},{1,7},{2,0},{3,1},{4,2},{5,3},{6,4},{7,5},{8,14},{9,15},{10,... | collective-permute-start | bytes 1751048 | tf_op jit(solution)/shard_map/ppermute | solution.py:31
  155.4 13.7 %collective-permute-done.37 = bf16[64,7296]{1,0:T(8,128)(2,1)S(1)} collective-permute-done((bf16[64,7296]{1,0:T(8,128)(2,1)S(1)}, bf16[64,7296]{1,0:T(8,128)(2,1)S(1)}, u32[]{:S(2)}, u32[]{:S(2)}) %collective-permute-start.37) | collective-permute-done | bytes 933920 | tf_op jit(solution)/shard_map/ppermute | solution.py:31
  169.1 1.6 fusion.15
  171.2 2.7 %collective-permute-start.20 = (bf16[16,7296]{1,0:T(8,128)(2,1)S(1)}, bf16[16,7296]{1,0:T(8,128)(2,1)S(1)}, u32[]{:S(2)}, u32[]{:S(2)}) collective-permute-start(bf16[16,7296]{1,0:T(8,128)(2,1)S(1)} %pad_maximum_fusion.27), channel_id=1, source_target_pairs={{0,6},{1,7},{2,0},{3,1},{4,2},{5,3},{6,4},{7,5},{8,14},{9,15},{10,... | collective-permute-start | bytes 700424 | tf_op jit(solution)/shard_map/ppermute | solution.py:31
  174.3 2.7 %collective-permute-start.41 = (bf16[40,7296]{1,0:T(8,128)(2,1)S(1)}, bf16[40,7296]{1,0:T(8,128)(2,1)S(1)}, u32[]{:S(2)}, u32[]{:S(2)}) collective-permute-start(bf16[40,7296]{1,0:T(8,128)(2,1)S(1)} %pad_maximum_fusion.19), channel_id=1, source_target_pairs={{0,6},{1,7},{2,0},{3,1},{4,2},{5,3},{6,4},{7,5},{8,14},{9,15},{10,... | collective-permute-start | bytes 1751048 | tf_op jit(solution)/shard_map/ppermute | solution.py:31
  177.0 1.3 collective-permute-done.19
  178.3 0.9 collective-permute-done.21
  179.2 1.2 fusion.23
  180.5 4.9 %collective-permute-start.22 = (bf16[16,7168]{1,0:T(8,128)(2,1)S(1)}, bf16[16,7168]{1,0:T(8,128)(2,1)S(1)}, u32[]{:S(2)}, u32[]{:S(2)}) collective-permute-start(bf16[16,7168]{1,0:T(8,128)(2,1)S(1)} %slice.478), channel_id=1, source_target_pairs={{32,0},{33,1},{34,2},{35,3},{36,4},{37,5},{38,6},{39,7},{40,8},{41... | collective-permute-start | bytes 688136 | tf_op jit(solution)/shard_map/ppermute | solution.py:38
  185.4 2.3 collective-permute-start.23
  188.5 1.6 collective-permute-done.41
  190.8 1.0 fusion.14
  193.1 2.3 collective-permute-start.43
  196.0 1.3 collective-permute-done.23.refs_1_
  198.0 7.0 %shard_map.96 = f32[128,7168]{1,0:T(8,128)} custom-call(bf16[128,7168]{1,0:T(8,128)(2,1)} %collective-permute-done.4.base_ref, f32[128,32]{1,0:T(8,128)} %bitcast.167, bf16[16,7168]{1,0:T(8,128)(2,1)} %copy-done.29, bf16[16,7168]{1,0:T(8,128)(2,1)} %copy-done.31), custom_call_target="tpu_custom_call" | custom-call | flops 24999999488 | bytes 7340032 | tf_op jit(solution)/shard_map/pallas_call | solution.py:305
  205.0 1.6 fusion.12
  206.6 1.1 collective-permute-start.48
  207.7 1.9 collective-permute-start.49
  209.6 4.3 %collective-permute-start.45 = (bf16[16,7168]{1,0:T(8,128)(2,1)S(1)}, bf16[16,7168]{1,0:T(8,128)(2,1)S(1)}, u32[]{:S(2)}, u32[]{:S(2)}) collective-permute-start(bf16[16,7168]{1,0:T(8,128)(2,1)S(1)} %slice.536), channel_id=1, source_target_pairs={{32,16},{33,17},{34,18},{35,19},{36,20},{37,21},{38,22},{39,23},{4... | collective-permute-start | bytes 688136 | tf_op jit(solution)/shard_map/ppermute | solution.py:38
  213.9 1.9 collective-permute-start.46
  216.7 6.0 %collective-permute-done.45 = bf16[16,7168]{1,0:T(8,128)(2,1)S(1)} collective-permute-done((bf16[16,7168]{1,0:T(8,128)(2,1)S(1)}, bf16[16,7168]{1,0:T(8,128)(2,1)S(1)}, u32[]{:S(2)}, u32[]{:S(2)}) %collective-permute-start.45) | collective-permute-done | bytes 229408 | tf_op jit(solution)/shard_map/ppermute | solution.py:38
  222.8 5.5 %collective-permute-done.46 = bf16[16,7168]{1,0:T(8,128)(2,1)S(1)} collective-permute-done((bf16[16,7168]{1,0:T(8,128)(2,1)S(1)}, bf16[16,7168]{1,0:T(8,128)(2,1)S(1)}, u32[]{:S(2)}, u32[]{:S(2)}) %collective-permute-start.46) | collective-permute-done | bytes 229408 | tf_op jit(solution)/shard_map/ppermute | solution.py:38
  229.0 1.3 copy-done.3
  230.3 2.1 fusion.3
  (192 shorter events, 18.4 us)
Async XLA Ops:
  4.1 8.4 %copy-start.24 = (s32[1,128,8]{1,2,0:T(8,128)S(1)}, s32[1,128,8]{1,2,0:T(8,128)}, u32[]{:S(2)}) copy-start(s32[1,128,8]{1,2,0:T(8,128)} %param.10) | copy-start | bytes 12292
  4.1 8.4 %copy-start.25 = (f32[1,128,8]{1,2,0:T(8,128)S(1)}, f32[1,128,8]{1,2,0:T(8,128)}, u32[]{:S(2)}) copy-start(f32[1,128,8]{1,2,0:T(8,128)} %param.11) | copy-start | bytes 12292
  4.2 12.6 %collective-permute-start.24 = (bf16[32,7168]{1,0:T(8,128)(2,1)S(1)}, bf16[32,7168]{1,0:T(8,128)(2,1)S(1)}, u32[]{:S(2)}, u32[]{:S(2)}) collective-permute-start(bf16[32,7168]{1,0:T(8,128)(2,1)S(1)} %pad_maximum_fusion.23), channel_id=1, source_target_pairs={{0,24},{1,25},{2,26},{3,27},{4,28},{5,29},{6,30},{7,31},{8,0},{9,1... | collective-permute-start | bytes 1376264 | tf_op jit(solution)/shard_map/ppermute | solution.py:31
  7.6 18.6 %copy-start.8 = (bf16[32,7168]{1,0:T(8,128)(2,1)}, bf16[32,7168]{1,0:T(8,128)(2,1)S(1)}, u32[]{:S(2)}) copy-start(bf16[32,7168]{1,0:T(8,128)(2,1)S(1)} %get-tuple-element.51.refs_0_) | copy-start | bytes 1376260
  7.6 12.5 %collective-permute-start.1 = (bf16[32,7168]{1,0:T(8,128)(2,1)S(1)}, bf16[32,7168]{1,0:T(8,128)(2,1)S(1)}, u32[]{:S(2)}, u32[]{:S(2)}) collective-permute-start(bf16[32,7168]{1,0:T(8,128)(2,1)S(1)} %get-tuple-element.51.refs_0_), channel_id=1, source_target_pairs={{0,2},{1,3},{2,4},{3,5},{4,6},{5,7},{6,0},{7,1},{8,10},{9,11},{10,... | collective-permute-start | bytes 1376264 | tf_op jit(solution)/shard_map/ppermute | solution.py:31
  9.0 12.8 %collective-permute-start.2 = (bf16[32,7168]{1,0:T(8,128)(2,1)S(1)}, bf16[32,7168]{1,0:T(8,128)(2,1)}, u32[]{:S(2)}, u32[]{:S(2)}) collective-permute-start(bf16[32,7168]{1,0:T(8,128)(2,1)S(1)} %get-tuple-element.51.refs_0_), channel_id=1, source_target_pairs={{0,1},{1,0},{2,3},{3,2},{4,5},{5,4},{6,7},{7,6},{8,9},{9,8},{10,11... | collective-permute-start | bytes 1376264 | tf_op jit(solution)/shard_map/ppermute | solution.py:31
  10.6 13.7 %collective-permute-start.3 = (bf16[32,7168]{1,0:T(8,128)(2,1)S(1)}, bf16[32,7168]{1,0:T(8,128)(2,1)}, u32[]{:S(2)}, u32[]{:S(2)}) collective-permute-start(bf16[32,7168]{1,0:T(8,128)(2,1)S(1)} %get-tuple-element.51.refs_0_), channel_id=1, source_target_pairs={{0,6},{1,7},{2,0},{3,1},{4,2},{5,3},{6,4},{7,5},{8,14},{9,15},{10,... | collective-permute-start | bytes 1376264 | tf_op jit(solution)/shard_map/ppermute | solution.py:31
  12.2 13.7 %collective-permute-start = (bf16[32,7168]{1,0:T(8,128)(2,1)S(1)}, bf16[32,7168]{1,0:T(8,128)(2,1)S(1)}, u32[]{:S(2)}, u32[]{:S(2)}) collective-permute-start(bf16[32,7168]{1,0:T(8,128)(2,1)S(1)} %pad_maximum_fusion.20), channel_id=1, source_target_pairs={{0,8},{1,9},{2,10},{3,11},{4,12},{5,13},{6,14},{7,15},{8,16},{9,17... | collective-permute-start | bytes 1376264 | tf_op jit(solution)/shard_map/ppermute | solution.py:31
  16.8 9.5 %copy-start.27 = (bf16[32,7168]{1,0:T(8,128)(2,1)}, bf16[32,7168]{1,0:T(8,128)(2,1)S(1)}, u32[]{:S(2)}) copy-start(bf16[32,7168]{1,0:T(8,128)(2,1)S(1)} %collective-permute-done.24.refs_0_) | copy-start | bytes 1376260
  16.8 13.4 %collective-permute-start.27 = (bf16[32,7168]{1,0:T(8,128)(2,1)S(1)}, bf16[32,7168]{1,0:T(8,128)(2,1)S(1)}, u32[]{:S(2)}, u32[]{:S(2)}) collective-permute-start(bf16[32,7168]{1,0:T(8,128)(2,1)S(1)} %collective-permute-done.24.refs_0_), channel_id=1, source_target_pairs={{0,2},{1,3},{2,4},{3,5},{4,6},{5,7},{6,0},{7,1},{8,10},{9,11},{10,... | collective-permute-start | bytes 1376264 | tf_op jit(solution)/shard_map/ppermute | solution.py:31
  20.1 11.4 %collective-permute-start.28 = (bf16[32,7168]{1,0:T(8,128)(2,1)S(1)}, bf16[32,7168]{1,0:T(8,128)(2,1)S(1)}, u32[]{:S(2)}, u32[]{:S(2)}) collective-permute-start(bf16[32,7168]{1,0:T(8,128)(2,1)S(1)} %collective-permute-done.24.refs_0_), channel_id=1, source_target_pairs={{0,1},{1,0},{2,3},{3,2},{4,5},{5,4},{6,7},{7,6},{8,9},{9,8},{10,11... | collective-permute-start | bytes 1376264 | tf_op jit(solution)/shard_map/ppermute | solution.py:31
  21.8 11.5 %collective-permute-start.25 = (bf16[32,7168]{1,0:T(8,128)(2,1)S(1)}, bf16[32,7168]{1,0:T(8,128)(2,1)S(1)}, u32[]{:S(2)}, u32[]{:S(2)}) collective-permute-start(bf16[32,7168]{1,0:T(8,128)(2,1)S(1)} %collective-permute-done.24.refs_0_), channel_id=1, source_target_pairs={{0,6},{1,7},{2,0},{3,1},{4,2},{5,3},{6,4},{7,5},{8,14},{9,15},{10,... | collective-permute-start | bytes 1376264 | tf_op jit(solution)/shard_map/ppermute | solution.py:31
  24.3 10.6 %collective-permute-start.26 = (bf16[32,7168]{1,0:T(8,128)(2,1)S(1)}, bf16[32,7168]{1,0:T(8,128)(2,1)S(1)}, u32[]{:S(2)}, u32[]{:S(2)}) collective-permute-start(bf16[32,7168]{1,0:T(8,128)(2,1)S(1)} %get-tuple-element.74), channel_id=1, source_target_pairs={{0,16},{1,17},{2,18},{3,19},{4,20},{5,21},{6,22},{7,23},{8,24},{9,... | collective-permute-start | bytes 1376264 | tf_op jit(solution)/shard_map/ppermute | solution.py:31
  26.7 25.9 %collective-permute-start.6 = (bf16[64,7168]{1,0:T(8,128)(2,1)S(1)}, bf16[64,7168]{1,0:T(8,128)(2,1)S(1)}, u32[]{:S(2)}, u32[]{:S(2)}) collective-permute-start(bf16[64,7168]{1,0:T(8,128)(2,1)S(1)} %get-tuple-element.55), channel_id=1, source_target_pairs={{0,2},{1,3},{2,4},{3,5},{4,6},{5,7},{6,0},{7,1},{8,10},{9,11},{10,... | collective-permute-start | bytes 2752520 | tf_op jit(solution)/shard_map/ppermute | solution.py:31
  30.1 4.8 %copy-start.9 = (bf16[32,7168]{1,0:T(8,128)(2,1)}, bf16[32,7168]{1,0:T(8,128)(2,1)S(1)}, u32[]{:S(2)}) copy-start(bf16[32,7168]{1,0:T(8,128)(2,1)S(1)} %collective-permute-done.27.refs_3_) | copy-start | bytes 1376260
  30.1 22.4 %collective-permute-start.7 = (bf16[64,7168]{1,0:T(8,128)(2,1)S(1)}, bf16[64,7168]{1,0:T(8,128)(2,1)S(1)}, u32[]{:S(2)}, u32[]{:S(2)}) collective-permute-start(bf16[64,7168]{1,0:T(8,128)(2,1)S(1)} %get-tuple-element.56), channel_id=1, source_target_pairs={{0,6},{1,7},{2,0},{3,1},{4,2},{5,3},{6,4},{7,5},{8,14},{9,15},{10,... | collective-permute-start | bytes 2752520 | tf_op jit(solution)/shard_map/ppermute | solution.py:31
  31.6 3.3 %copy-start.17 = (bf16[32,7168]{1,0:T(8,128)(2,1)}, bf16[32,7168]{1,0:T(8,128)(2,1)S(1)}, u32[]{:S(2)}) copy-start(bf16[32,7168]{1,0:T(8,128)(2,1)S(1)} %collective-permute-done.28.refs_4_) | copy-start | bytes 1376260
  31.6 21.1 %collective-permute-start.8 = (bf16[64,7168]{1,0:T(8,128)(2,1)S(1)}, bf16[64,7168]{1,0:T(8,128)(2,1)S(1)}, u32[]{:S(2)}, u32[]{:S(2)}) collective-permute-start(bf16[64,7168]{1,0:T(8,128)(2,1)S(1)} %get-tuple-element.57), channel_id=1, source_target_pairs={{0,1},{1,0},{2,3},{3,2},{4,5},{5,4},{6,7},{7,6},{8,9},{9,8},{10,11... | collective-permute-start | bytes 2752520 | tf_op jit(solution)/shard_map/ppermute | solution.py:31
  35.7 36.6 %collective-permute-start.29 = (bf16[64,7168]{1,0:T(8,128)(2,1)S(1)}, bf16[64,7168]{1,0:T(8,128)(2,1)S(1)}, u32[]{:S(2)}, u32[]{:S(2)}) collective-permute-start(bf16[64,7168]{1,0:T(8,128)(2,1)S(1)} %get-tuple-element.77), channel_id=1, source_target_pairs={{0,2},{1,3},{2,4},{3,5},{4,6},{5,7},{6,0},{7,1},{8,10},{9,11},{10,... | collective-permute-start | bytes 2752520 | tf_op jit(solution)/shard_map/ppermute | solution.py:31
  35.7 36.5 %collective-permute-start.30 = (bf16[64,7168]{1,0:T(8,128)(2,1)S(1)}, bf16[64,7168]{1,0:T(8,128)(2,1)S(1)}, u32[]{:S(2)}, u32[]{:S(2)}) collective-permute-start(bf16[64,7168]{1,0:T(8,128)(2,1)S(1)} %get-tuple-element.78), channel_id=1, source_target_pairs={{0,6},{1,7},{2,0},{3,1},{4,2},{5,3},{6,4},{7,5},{8,14},{9,15},{10,... | collective-permute-start | bytes 2752520 | tf_op jit(solution)/shard_map/ppermute | solution.py:31
  52.6 19.8 %collective-permute-start.31 = (bf16[64,7168]{1,0:T(8,128)(2,1)S(1)}, bf16[64,7168]{1,0:T(8,128)(2,1)S(1)}, u32[]{:S(2)}, u32[]{:S(2)}) collective-permute-start(bf16[64,7168]{1,0:T(8,128)(2,1)S(1)} %get-tuple-element.79), channel_id=1, source_target_pairs={{0,1},{1,0},{2,3},{3,2},{4,5},{5,4},{6,7},{7,6},{8,9},{9,8},{10,11... | collective-permute-start | bytes 2752520 | tf_op jit(solution)/shard_map/ppermute | solution.py:31
  54.1 28.9 %collective-permute-start.9 = (bf16[48,7168]{1,0:T(8,128)(2,1)S(1)}, bf16[48,7168]{1,0:T(8,128)(2,1)S(1)}, u32[]{:S(2)}, u32[]{:S(2)}) collective-permute-start(bf16[48,7168]{1,0:T(8,128)(2,1)S(1)} %get-tuple-element.58), channel_id=1, source_target_pairs={{0,2},{1,3},{2,4},{3,5},{4,6},{5,7},{6,0},{7,1},{8,10},{9,11},{10,... | collective-permute-start | bytes 2064392 | tf_op jit(solution)/shard_map/ppermute | solution.py:31
  54.1 32.9 %collective-permute-start.10 = (bf16[48,7168]{1,0:T(8,128)(2,1)S(1)}, bf16[48,7168]{1,0:T(8,128)(2,1)S(1)}, u32[]{:S(2)}, u32[]{:S(2)}) collective-permute-start(bf16[48,7168]{1,0:T(8,128)(2,1)S(1)} %get-tuple-element.59), channel_id=1, source_target_pairs={{0,6},{1,7},{2,0},{3,1},{4,2},{5,3},{6,4},{7,5},{8,14},{9,15},{10,... | collective-permute-start | bytes 2064392 | tf_op jit(solution)/shard_map/ppermute | solution.py:31
  72.2 8.4 %collective-permute-start.11 = (bf16[32,7168]{1,0:T(8,128)(2,1)S(1)}, bf16[32,7168]{1,0:T(8,128)(2,1)S(1)}, u32[]{:S(2)}, u32[]{:S(2)}) collective-permute-start(bf16[32,7168]{1,0:T(8,128)(2,1)S(1)} %pad_maximum_fusion.22), channel_id=1, source_target_pairs={{0,1},{1,0},{2,3},{3,2},{4,5},{5,4},{6,7},{7,6},{8,9},{9,8},{10,11... | collective-permute-start | bytes 1376264 | tf_op jit(solution)/shard_map/ppermute | solution.py:31
  73.7 23.7 %collective-permute-start.34 = (bf16[32,7168]{1,0:T(8,128)(2,1)S(1)}, bf16[32,7168]{1,0:T(8,128)(2,1)S(1)}, u32[]{:S(2)}, u32[]{:S(2)}) collective-permute-start(bf16[32,7168]{1,0:T(8,128)(2,1)S(1)} %pad_maximum_fusion.25), channel_id=1, source_target_pairs={{0,1},{1,0},{2,3},{3,2},{4,5},{5,4},{6,7},{7,6},{8,9},{9,8},{10,11... | collective-permute-start | bytes 1376264 | tf_op jit(solution)/shard_map/ppermute | solution.py:31
  80.6 19.9 %copy-start.20 = (bf16[32,7168]{1,0:T(8,128)(2,1)}, bf16[32,7168]{1,0:T(8,128)(2,1)S(1)}, u32[]{:S(2)}) copy-start(bf16[32,7168]{1,0:T(8,128)(2,1)S(1)} %collective-permute-done.11.refs_11_) | copy-start | bytes 1376260
  83.0 3.9 %copy-start.21 = (bf16[48,7168]{1,0:T(8,128)(2,1)}, bf16[48,7168]{1,0:T(8,128)(2,1)S(1)}, u32[]{:S(2)}) copy-start(bf16[48,7168]{1,0:T(8,128)(2,1)S(1)} %collective-permute-done.9.refs_6_) | copy-start | bytes 2064388
  87.0 10.6 %collective-permute-start.12 = (bf16[16,7168]{1,0:T(8,128)(2,1)S(1)}, bf16[16,7168]{1,0:T(8,128)(2,1)}, u32[]{:S(2)}, u32[]{:S(2)}) collective-permute-start(bf16[16,7168]{1,0:T(8,128)(2,1)S(1)} %slice.447), channel_id=1, source_target_pairs={{0,2},{1,3},{2,4},{3,5},{4,6},{5,7},{6,0},{7,1},{8,10},{9,11},{10,... | collective-permute-start | bytes 688136 | tf_op jit(solution)/shard_map/ppermute | solution.py:31
  87.8 12.7 %collective-permute-start.13 = (bf16[16,7168]{1,0:T(8,128)(2,1)S(1)}, bf16[16,7168]{1,0:T(8,128)(2,1)}, u32[]{:S(2)}, u32[]{:S(2)}) collective-permute-start(bf16[16,7168]{1,0:T(8,128)(2,1)S(1)} %slice.448), channel_id=1, source_target_pairs={{0,6},{1,7},{2,0},{3,1},{4,2},{5,3},{6,4},{7,5},{8,14},{9,15},{10,... | collective-permute-start | bytes 688136 | tf_op jit(solution)/shard_map/ppermute | solution.py:31
  90.2 33.2 %collective-permute-start.4 = (bf16[128,7168]{1,0:T(8,128)(2,1)}, bf16[128,7168]{1,0:T(8,128)(2,1)}, u32[]{:S(2)}, u32[]{:S(2)}) collective-permute-start(bf16[128,7168]{1,0:T(8,128)(2,1)} %bitcast.166), channel_id=1, source_target_pairs={{32,0},{33,1},{34,2},{35,3},{36,4},{37,5},{38,6},{39,7},{40,8},{41... | collective-permute-start | bytes 5505032 | tf_op jit(solution)/shard_map/ppermute | solution.py:38
  95.5 28.0 %collective-permute-start.5 = (f32[128,64]{1,0:T(8,128)S(1)}, f32[128,64]{1,0:T(8,128)S(1)}, u32[]{:S(2)}, u32[]{:S(2)}) collective-permute-start(f32[128,64]{1,0:T(8,128)S(1)} %and_select_fusion), channel_id=1, source_target_pairs={{32,0},{33,1},{34,2},{35,3},{36,4},{37,5},{38,6},{39,7},{40,8},{41... | collective-permute-start | bytes 98312 | tf_op jit(solution)/shard_map/ppermute | solution.py:38
  97.4 18.8 %copy-start.19 = (bf16[32,7168]{1,0:T(8,128)(2,1)}, bf16[32,7168]{1,0:T(8,128)(2,1)S(1)}, u32[]{:S(2)}) copy-start(bf16[32,7168]{1,0:T(8,128)(2,1)S(1)} %collective-permute-done.34.refs_11_) | copy-start | bytes 1376260
  97.5 21.3 %collective-permute-start.32 = (bf16[48,7168]{1,0:T(8,128)(2,1)S(1)}, bf16[48,7168]{1,0:T(8,128)(2,1)}, u32[]{:S(2)}, u32[]{:S(2)}) collective-permute-start(bf16[48,7168]{1,0:T(8,128)(2,1)S(1)} %get-tuple-element.80), channel_id=1, source_target_pairs={{0,2},{1,3},{2,4},{3,5},{4,6},{5,7},{6,0},{7,1},{8,10},{9,11},{10,... | collective-permute-start | bytes 2064392 | tf_op jit(solution)/shard_map/ppermute | solution.py:31
  97.6 22.1 %collective-permute-start.33 = (bf16[48,7168]{1,0:T(8,128)(2,1)S(1)}, bf16[48,7168]{1,0:T(8,128)(2,1)}, u32[]{:S(2)}, u32[]{:S(2)}) collective-permute-start(bf16[48,7168]{1,0:T(8,128)(2,1)S(1)} %get-tuple-element.81), channel_id=1, source_target_pairs={{0,6},{1,7},{2,0},{3,1},{4,2},{5,3},{6,4},{7,5},{8,14},{9,15},{10,... | collective-permute-start | bytes 2064392 | tf_op jit(solution)/shard_map/ppermute | solution.py:31
  119.7 8.4 %collective-permute-start.35 = (bf16[16,7168]{1,0:T(8,128)(2,1)S(1)}, bf16[16,7168]{1,0:T(8,128)(2,1)S(1)}, u32[]{:S(2)}, u32[]{:S(2)}) collective-permute-start(bf16[16,7168]{1,0:T(8,128)(2,1)S(1)} %slice.499), channel_id=1, source_target_pairs={{0,2},{1,3},{2,4},{3,5},{4,6},{5,7},{6,0},{7,1},{8,10},{9,11},{10,... | collective-permute-start | bytes 688136 | tf_op jit(solution)/shard_map/ppermute | solution.py:31
  119.8 8.4 %collective-permute-start.36 = (bf16[16,7168]{1,0:T(8,128)(2,1)S(1)}, bf16[16,7168]{1,0:T(8,128)(2,1)S(1)}, u32[]{:S(2)}, u32[]{:S(2)}) collective-permute-start(bf16[16,7168]{1,0:T(8,128)(2,1)S(1)} %slice.500), channel_id=1, source_target_pairs={{0,6},{1,7},{2,0},{3,1},{4,2},{5,3},{6,4},{7,5},{8,14},{9,15},{10,... | collective-permute-start | bytes 688136 | tf_op jit(solution)/shard_map/ppermute | solution.py:31
  123.5 21.8 %copy-start.13 = (f32[128,64]{1,0:T(8,128)}, f32[128,64]{1,0:T(8,128)S(1)}, u32[]{:S(2)}) copy-start(f32[128,64]{1,0:T(8,128)S(1)} %collective-permute-done.5) | copy-start | bytes 98308
  123.5 26.8 %collective-permute-start.14 = (bf16[64,7296]{1,0:T(8,128)(2,1)}, bf16[64,7296]{1,0:T(8,128)(2,1)}, u32[]{:S(2)}, u32[]{:S(2)}) collective-permute-start(bf16[64,7296]{1,0:T(8,128)(2,1)} %pad_maximum_fusion.8), channel_id=1, source_target_pairs={{0,1},{1,0},{2,3},{3,2},{4,5},{5,4},{6,7},{7,6},{8,9},{9,8},{10,11... | collective-permute-start | bytes 2801672 | tf_op jit(solution)/shard_map/ppermute | solution.py:31
  124.0 23.7 %collective-permute-start.15 = (bf16[16,7296]{1,0:T(8,128)(2,1)}, bf16[16,7296]{1,0:T(8,128)(2,1)S(1)}, u32[]{:S(2)}, u32[]{:S(2)}) collective-permute-start(bf16[16,7296]{1,0:T(8,128)(2,1)} %get-tuple-element.64), channel_id=1, source_target_pairs={{0,2},{1,3},{2,4},{3,5},{4,6},{5,7},{6,0},{7,1},{8,10},{9,11},{10,... | collective-permute-start | bytes 700424 | tf_op jit(solution)/shard_map/ppermute | solution.py:31
  124.0 26.4 %collective-permute-start.16 = (bf16[16,7296]{1,0:T(8,128)(2,1)}, bf16[16,7296]{1,0:T(8,128)(2,1)S(1)}, u32[]{:S(2)}, u32[]{:S(2)}) collective-permute-start(bf16[16,7296]{1,0:T(8,128)(2,1)} %get-tuple-element.65), channel_id=1, source_target_pairs={{0,6},{1,7},{2,0},{3,1},{4,2},{5,3},{6,4},{7,5},{8,14},{9,15},{10,... | collective-permute-start | bytes 700424 | tf_op jit(solution)/shard_map/ppermute | solution.py:31
  145.3 5.1 %copy-start.2 = (bf16[256,7296]{1,0:T(8,128)(2,1)S(1)}, bf16[256,7296]{1,0:T(8,128)(2,1)}, u32[]{:S(2)}) copy-start(bf16[256,7296]{1,0:T(8,128)(2,1)} %shard_map.95) | copy-start | bytes 11206660
  147.2 22.0 %collective-permute-start.37 = (bf16[64,7296]{1,0:T(8,128)(2,1)S(1)}, bf16[64,7296]{1,0:T(8,128)(2,1)S(1)}, u32[]{:S(2)}, u32[]{:S(2)}) collective-permute-start(bf16[64,7296]{1,0:T(8,128)(2,1)S(1)} %pad_maximum_fusion.9), channel_id=1, source_target_pairs={{0,1},{1,0},{2,3},{3,2},{4,5},{5,4},{6,7},{7,6},{8,9},{9,8},{10,11... | collective-permute-start | bytes 2801672 | tf_op jit(solution)/shard_map/ppermute | solution.py:31
  147.6 7.8 %collective-permute-start.38 = (bf16[16,7296]{1,0:T(8,128)(2,1)S(1)}, bf16[16,7296]{1,0:T(8,128)(2,1)S(1)}, u32[]{:S(2)}, u32[]{:S(2)}) collective-permute-start(bf16[16,7296]{1,0:T(8,128)(2,1)S(1)} %get-tuple-element.86), channel_id=1, source_target_pairs={{0,2},{1,3},{2,4},{3,5},{4,6},{5,7},{6,0},{7,1},{8,10},{9,11},{10,... | collective-permute-start | bytes 700424 | tf_op jit(solution)/shard_map/ppermute | solution.py:31
  147.6 7.8 %collective-permute-start.39 = (bf16[16,7296]{1,0:T(8,128)(2,1)S(1)}, bf16[16,7296]{1,0:T(8,128)(2,1)S(1)}, u32[]{:S(2)}, u32[]{:S(2)}) collective-permute-start(bf16[16,7296]{1,0:T(8,128)(2,1)S(1)} %get-tuple-element.87), channel_id=1, source_target_pairs={{0,6},{1,7},{2,0},{3,1},{4,2},{5,3},{6,4},{7,5},{8,14},{9,15},{10,... | collective-permute-start | bytes 700424 | tf_op jit(solution)/shard_map/ppermute | solution.py:31
  151.9 19.0 %collective-permute-start.17 = (bf16[40,7296]{1,0:T(8,128)(2,1)S(1)}, bf16[40,7296]{1,0:T(8,128)(2,1)S(1)}, u32[]{:S(2)}, u32[]{:S(2)}) collective-permute-start(bf16[40,7296]{1,0:T(8,128)(2,1)S(1)} %pad_maximum_fusion.16), channel_id=1, source_target_pairs={{0,2},{1,3},{2,4},{3,5},{4,6},{5,7},{6,0},{7,1},{8,10},{9,11},{10,... | collective-permute-start | bytes 1751048 | tf_op jit(solution)/shard_map/ppermute | solution.py:31
  152.0 18.9 %collective-permute-start.18 = (bf16[40,7296]{1,0:T(8,128)(2,1)S(1)}, bf16[40,7296]{1,0:T(8,128)(2,1)S(1)}, u32[]{:S(2)}, u32[]{:S(2)}) collective-permute-start(bf16[40,7296]{1,0:T(8,128)(2,1)S(1)} %pad_maximum_fusion.17), channel_id=1, source_target_pairs={{0,6},{1,7},{2,0},{3,1},{4,2},{5,3},{6,4},{7,5},{8,14},{9,15},{10,... | collective-permute-start | bytes 1751048 | tf_op jit(solution)/shard_map/ppermute | solution.py:31
  171.1 7.2 %collective-permute-start.19 = (bf16[16,7296]{1,0:T(8,128)(2,1)S(1)}, bf16[16,7296]{1,0:T(8,128)(2,1)S(1)}, u32[]{:S(2)}, u32[]{:S(2)}) collective-permute-start(bf16[16,7296]{1,0:T(8,128)(2,1)S(1)} %pad_maximum_fusion.26), channel_id=1, source_target_pairs={{0,2},{1,3},{2,4},{3,5},{4,6},{5,7},{6,0},{7,1},{8,10},{9,11},{10,... | collective-permute-start | bytes 700424 | tf_op jit(solution)/shard_map/ppermute | solution.py:31
  171.2 7.2 %collective-permute-start.20 = (bf16[16,7296]{1,0:T(8,128)(2,1)S(1)}, bf16[16,7296]{1,0:T(8,128)(2,1)S(1)}, u32[]{:S(2)}, u32[]{:S(2)}) collective-permute-start(bf16[16,7296]{1,0:T(8,128)(2,1)S(1)} %pad_maximum_fusion.27), channel_id=1, source_target_pairs={{0,6},{1,7},{2,0},{3,1},{4,2},{5,3},{6,4},{7,5},{8,14},{9,15},{10,... | collective-permute-start | bytes 700424 | tf_op jit(solution)/shard_map/ppermute | solution.py:31
  173.8 5.4 %collective-permute-start.21 = (bf16[16,7296]{1,0:T(8,128)(2,1)S(1)}, bf16[16,7296]{1,0:T(8,128)(2,1)S(1)}, u32[]{:S(2)}, u32[]{:S(2)}) collective-permute-start(bf16[16,7296]{1,0:T(8,128)(2,1)S(1)} %fusion.25), channel_id=1, source_target_pairs={{0,1},{1,0},{2,3},{3,2},{4,5},{5,4},{6,7},{7,6},{8,9},{9,8},{10,11... | collective-permute-start | bytes 700424 | tf_op jit(solution)/shard_map/ppermute | solution.py:31
  174.3 16.6 %collective-permute-start.40 = (bf16[40,7296]{1,0:T(8,128)(2,1)S(1)}, bf16[40,7296]{1,0:T(8,128)(2,1)S(1)}, u32[]{:S(2)}, u32[]{:S(2)}) collective-permute-start(bf16[40,7296]{1,0:T(8,128)(2,1)S(1)} %pad_maximum_fusion.18), channel_id=1, source_target_pairs={{0,2},{1,3},{2,4},{3,5},{4,6},{5,7},{6,0},{7,1},{8,10},{9,11},{10,... | collective-permute-start | bytes 1751048 | tf_op jit(solution)/shard_map/ppermute | solution.py:31
  174.3 15.7 %collective-permute-start.41 = (bf16[40,7296]{1,0:T(8,128)(2,1)S(1)}, bf16[40,7296]{1,0:T(8,128)(2,1)S(1)}, u32[]{:S(2)}, u32[]{:S(2)}) collective-permute-start(bf16[40,7296]{1,0:T(8,128)(2,1)S(1)} %pad_maximum_fusion.19), channel_id=1, source_target_pairs={{0,6},{1,7},{2,0},{3,1},{4,2},{5,3},{6,4},{7,5},{8,14},{9,15},{10,... | collective-permute-start | bytes 1751048 | tf_op jit(solution)/shard_map/ppermute | solution.py:31
  180.5 14.8 %collective-permute-start.22 = (bf16[16,7168]{1,0:T(8,128)(2,1)S(1)}, bf16[16,7168]{1,0:T(8,128)(2,1)S(1)}, u32[]{:S(2)}, u32[]{:S(2)}) collective-permute-start(bf16[16,7168]{1,0:T(8,128)(2,1)S(1)} %slice.478), channel_id=1, source_target_pairs={{32,0},{33,1},{34,2},{35,3},{36,4},{37,5},{38,6},{39,7},{40,8},{41... | collective-permute-start | bytes 688136 | tf_op jit(solution)/shard_map/ppermute | solution.py:38
  185.4 11.9 %collective-permute-start.23 = (bf16[16,7168]{1,0:T(8,128)(2,1)S(1)}, bf16[16,7168]{1,0:T(8,128)(2,1)S(1)}, u32[]{:S(2)}, u32[]{:S(2)}) collective-permute-start(bf16[16,7168]{1,0:T(8,128)(2,1)S(1)} %slice.483), channel_id=1, source_target_pairs={{32,24},{33,25},{34,26},{35,27},{36,28},{37,29},{38,30},{39,31},{4... | collective-permute-start | bytes 688136 | tf_op jit(solution)/shard_map/ppermute | solution.py:38
  187.7 28.2 %collective-permute-start.47 = (bf16[16,128]{1,0:T(8,128)(2,1)S(1)}, bf16[16,128]{1,0:T(8,128)(2,1)S(1)}, u32[]{:S(2)}, u32[]{:S(2)}) collective-permute-start(bf16[16,128]{1,0:T(8,128)(2,1)S(1)} %slice.482), channel_id=1, source_target_pairs={{0,24},{1,25},{2,26},{3,27},{4,28},{5,29},{6,30},{7,31},{8,0},{9,1... | collective-permute-start | bytes 12296 | tf_op jit(solution)/shard_map/ppermute | solution.py:31
  192.6 12.3 %collective-permute-start.42 = (bf16[16,7296]{1,0:T(8,128)(2,1)}, bf16[16,7296]{1,0:T(8,128)(2,1)S(1)}, u32[]{:S(2)}, u32[]{:S(2)}) collective-permute-start(bf16[16,7296]{1,0:T(8,128)(2,1)} %pad_maximum_fusion.28), channel_id=1, source_target_pairs={{0,2},{1,3},{2,4},{3,5},{4,6},{5,7},{6,0},{7,1},{8,10},{9,11},{10,... | collective-permute-start | bytes 700424 | tf_op jit(solution)/shard_map/ppermute | solution.py:31
  193.1 11.9 %collective-permute-start.43 = (bf16[16,7296]{1,0:T(8,128)(2,1)S(1)}, bf16[16,7296]{1,0:T(8,128)(2,1)S(1)}, u32[]{:S(2)}, u32[]{:S(2)}) collective-permute-start(bf16[16,7296]{1,0:T(8,128)(2,1)S(1)} %pad_maximum_fusion.29), channel_id=1, source_target_pairs={{0,6},{1,7},{2,0},{3,1},{4,2},{5,3},{6,4},{7,5},{8,14},{9,15},{10,... | collective-permute-start | bytes 700424 | tf_op jit(solution)/shard_map/ppermute | solution.py:31
  195.3 9.6 %collective-permute-start.44 = (bf16[16,7296]{1,0:T(8,128)(2,1)S(1)}, bf16[16,7296]{1,0:T(8,128)(2,1)}, u32[]{:S(2)}, u32[]{:S(2)}) collective-permute-start(bf16[16,7296]{1,0:T(8,128)(2,1)S(1)} %fusion.14), channel_id=1, source_target_pairs={{0,1},{1,0},{2,3},{3,2},{4,5},{5,4},{6,7},{7,6},{8,9},{9,8},{10,11... | collective-permute-start | bytes 700424 | tf_op jit(solution)/shard_map/ppermute | solution.py:31
  204.9 23.3 %copy-start.14 = (f32[128,64]{1,0:T(8,128)S(1)}, f32[128,64]{1,0:T(8,128)}, u32[]{:S(2)}) copy-start(f32[128,64]{1,0:T(8,128)} %copy-done.13) | copy-start | bytes 98308
  205.0 24.0 %copy-start.5 = (bf16[128,7168]{1,0:T(8,128)(2,1)S(1)}, bf16[128,7168]{1,0:T(8,128)(2,1)}, u32[]{:S(2)}) copy-start(bf16[128,7168]{1,0:T(8,128)(2,1)} %param.15) | copy-start | bytes 5505028
  206.6 9.2 %collective-permute-start.48 = (bf16[16,128]{1,0:T(8,128)(2,1)S(1)}, bf16[16,128]{1,0:T(8,128)(2,1)S(1)}, u32[]{:S(2)}, u32[]{:S(2)}) collective-permute-start(bf16[16,128]{1,0:T(8,128)(2,1)S(1)} %slice.535), channel_id=1, source_target_pairs={{0,16},{1,17},{2,18},{3,19},{4,20},{5,21},{6,22},{7,23},{8,24},{9,... | collective-permute-start | bytes 12296 | tf_op jit(solution)/shard_map/ppermute | solution.py:31
  207.7 8.1 %collective-permute-start.49 = (bf16[16,128]{1,0:T(8,128)(2,1)S(1)}, bf16[16,128]{1,0:T(8,128)(2,1)S(1)}, u32[]{:S(2)}, u32[]{:S(2)}) collective-permute-start(bf16[16,128]{1,0:T(8,128)(2,1)S(1)} %slice.530), channel_id=1, source_target_pairs={{0,8},{1,9},{2,10},{3,11},{4,12},{5,13},{6,14},{7,15},{8,16},{9,17... | collective-permute-start | bytes 12296 | tf_op jit(solution)/shard_map/ppermute | solution.py:31
  209.6 13.1 %collective-permute-start.45 = (bf16[16,7168]{1,0:T(8,128)(2,1)S(1)}, bf16[16,7168]{1,0:T(8,128)(2,1)S(1)}, u32[]{:S(2)}, u32[]{:S(2)}) collective-permute-start(bf16[16,7168]{1,0:T(8,128)(2,1)S(1)} %slice.536), channel_id=1, source_target_pairs={{32,16},{33,17},{34,18},{35,19},{36,20},{37,21},{38,22},{39,23},{4... | collective-permute-start | bytes 688136 | tf_op jit(solution)/shard_map/ppermute | solution.py:38
  213.9 14.3 %collective-permute-start.46 = (bf16[16,7168]{1,0:T(8,128)(2,1)S(1)}, bf16[16,7168]{1,0:T(8,128)(2,1)S(1)}, u32[]{:S(2)}, u32[]{:S(2)}) collective-permute-start(bf16[16,7168]{1,0:T(8,128)(2,1)S(1)} %slice.531), channel_id=1, source_target_pairs={{32,8},{33,9},{34,10},{35,11},{36,12},{37,13},{38,14},{39,15},{40,... | collective-permute-start | bytes 688136 | tf_op jit(solution)/shard_map/ppermute | solution.py:38
  230.3 2.1 copy-start.1
  (18 other events, 21.9 us)

commit v2 on v1

--- a/solution.py
+++ b/solution.py
@@ -210,7 +210,7 @@
     grad_plan = [(index_of(arrays, a), r) for a, r in grad_pieces]
     depth, units = gate_mat.shape
     rows = len(in_pieces) * CAP
-    step = 1024 if depth % 1024 == 0 else 128
+    step = 1792 if depth % 1792 == 0 else 128
 
     def kernel(piece_ref, *refs):
         ins = refs[: len(arrays)]

time: 233 us -> 231 us (level)
  transfers between devices with their start and end apart: 50 -> 50, of which waited for: 19 -> 19; matrix products, arithmetic and copies ran while one was open for 8% -> 8% of each run, Pallas kernels for 17% -> 16%
where the time goes in v2:
time: 231 us
  waiting for transfers between devices  85.7 us (37%)
  starting transfers between devices  73.7 us (32%)
  Pallas kernels  36.6 us (16%)
  local copies, waits for them, and re-layouts  17.2 us (7%)
  other arithmetic  12.2 us (5%)
  matrix products  3.52 us (2%)
    ppermute x44, waiting for transfers between devices, send(): return lax.ppermute(block, 'expert', route)  72.9 us
    ppermute x44, starting transfers between devices, send(): return lax.ppermute(block, 'expert', route)  53.1 us
    pallas_call x2, Pallas kernels, experts_backward(): pl.pallas_call(kernel, out_shape=jax.ShapeDtypeStruct((rows, depth + MARK...  29.6 us
    ppermute x6, starting transfers between devices, send(): return lax.ppermute(block, ('pipe', 'expert'), route)  20.6 us
    ppermute x6, waiting for transfers between devices, send(): return lax.ppermute(block, ('pipe', 'expert'), route)  12.8 us
    unnamed x65, local copies, waits for them, and re-layouts  8.86 us
    convert_element_type x10, other arithmetic, added(): return total.astype(jnp.bfloat16)  7.07 us
    pallas_call x1, Pallas kernels, blend(): pl.pallas_call(kernel, grid=(width // step,), out_shape=jax.ShapeDtypeStr...  6.98 us
  transfers between devices with their start and end apart: 50, of which 19 were waited for; matrix products, arithmetic and copies ran while one was open for 8% of the time, Pallas kernels for 16%

profile of v2, /device:TPU:1, one launch (start us, length us, event | category | flops | bytes accessed | tf_op | source)
XLA Modules:
  0.0 230.6 jit_solution(15426092320777276495)
XLA Ops:
  0.7 0.9 compare_reduce_fusion
  2.6 1.0 copy-done.4
  4.2 3.4 %collective-permute-start.24 = (bf16[32,7168]{1,0:T(8,128)(2,1)S(1)}, bf16[32,7168]{1,0:T(8,128)(2,1)S(1)}, u32[]{:S(2)}, u32[]{:S(2)}) collective-permute-start(bf16[32,7168]{1,0:T(8,128)(2,1)S(1)} %pad_maximum_fusion.23), channel_id=1, source_target_pairs={{0,24},{1,25},{2,26},{3,27},{4,28},{5,29},{6,30},{7,31},{8,0},{9,1... | collective-permute-start | bytes 1376264 | tf_op jit(solution)/shard_map/ppermute | solution.py:31
  7.6 1.4 collective-permute-start.1
  9.0 1.6 collective-permute-start.2
  10.6 1.5 collective-permute-start.3
  12.9 3.9 %collective-permute-done.24.refs_0_ = bf16[32,7168]{1,0:T(8,128)(2,1)S(1)} collective-permute-done((bf16[32,7168]{1,0:T(8,128)(2,1)S(1)}, bf16[32,7168]{1,0:T(8,128)(2,1)S(1)}, u32[]{:S(2)}, u32[]{:S(2)}) %collective-permute-start.24) | collective-permute-done | bytes 458784 | tf_op jit(solution)/shard_map/ppermute | solution.py:31
  16.8 1.3 collective-permute-start.27
  18.0 2.1 collective-permute-done.1.refs_3_
  20.1 1.7 collective-permute-start.28
  21.8 1.6 collective-permute-start.25
  23.4 1.0 slice.437
  25.0 1.0 slice.438
  26.7 3.4 %collective-permute-done.27.refs_3_ = bf16[32,7168]{1,0:T(8,128)(2,1)S(1)} collective-permute-done((bf16[32,7168]{1,0:T(8,128)(2,1)S(1)}, bf16[32,7168]{1,0:T(8,128)(2,1)S(1)}, u32[]{:S(2)}, u32[]{:S(2)}) %collective-permute-start.27) | collective-permute-done | bytes 458784 | tf_op jit(solution)/shard_map/ppermute | solution.py:31
  30.1 1.4 collective-permute-start.7
  31.6 1.7 collective-permute-start.8
  33.4 1.5 collective-permute-done.26.refs_7_
  35.7 2.7 %collective-permute-start.30 = (bf16[64,7168]{1,0:T(8,128)(2,1)S(1)}, bf16[64,7168]{1,0:T(8,128)(2,1)S(1)}, u32[]{:S(2)}, u32[]{:S(2)}) collective-permute-start(bf16[64,7168]{1,0:T(8,128)(2,1)S(1)} %get-tuple-element.78), channel_id=1, source_target_pairs={{0,6},{1,7},{2,0},{3,1},{4,2},{5,3},{6,4},{7,5},{8,14},{9,15},{10,... | collective-permute-start | bytes 2752520 | tf_op jit(solution)/shard_map/ppermute | solution.py:31
  38.4 14.2 %collective-permute-done.7.refs_5_ = bf16[64,7168]{1,0:T(8,128)(2,1)S(1)} collective-permute-done((bf16[64,7168]{1,0:T(8,128)(2,1)S(1)}, bf16[64,7168]{1,0:T(8,128)(2,1)S(1)}, u32[]{:S(2)}, u32[]{:S(2)}) %collective-permute-start.7) | collective-permute-done | bytes 917536 | tf_op jit(solution)/shard_map/ppermute | solution.py:31
  54.1 2.7 %collective-permute-start.10 = (bf16[48,7168]{1,0:T(8,128)(2,1)S(1)}, bf16[48,7168]{1,0:T(8,128)(2,1)S(1)}, u32[]{:S(2)}, u32[]{:S(2)}) collective-permute-start(bf16[48,7168]{1,0:T(8,128)(2,1)S(1)} %get-tuple-element.59), channel_id=1, source_target_pairs={{0,6},{1,7},{2,0},{3,1},{4,2},{5,3},{6,4},{7,5},{8,14},{9,15},{10,... | collective-permute-start | bytes 2064392 | tf_op jit(solution)/shard_map/ppermute | solution.py:31
  56.8 15.4 %collective-permute-done.30.refs_5_ = bf16[64,7168]{1,0:T(8,128)(2,1)S(1)} collective-permute-done((bf16[64,7168]{1,0:T(8,128)(2,1)S(1)}, bf16[64,7168]{1,0:T(8,128)(2,1)S(1)}, u32[]{:S(2)}, u32[]{:S(2)}) %collective-permute-start.30) | collective-permute-done | bytes 917536 | tf_op jit(solution)/shard_map/ppermute | solution.py:31
  73.7 1.2 collective-permute-start.34
  75.0 5.7 %collective-permute-done.11.refs_11_ = bf16[32,7168]{1,0:T(8,128)(2,1)S(1)} collective-permute-done((bf16[32,7168]{1,0:T(8,128)(2,1)S(1)}, bf16[32,7168]{1,0:T(8,128)(2,1)S(1)}, u32[]{:S(2)}, u32[]{:S(2)}) %collective-permute-start.11) | collective-permute-done | bytes 458784 | tf_op jit(solution)/shard_map/ppermute | solution.py:31
  80.6 2.4 %collective-permute-done.9.refs_6_ = bf16[48,7168]{1,0:T(8,128)(2,1)S(1)} collective-permute-done((bf16[48,7168]{1,0:T(8,128)(2,1)S(1)}, bf16[48,7168]{1,0:T(8,128)(2,1)S(1)}, u32[]{:S(2)}, u32[]{:S(2)}) %collective-permute-start.9) | collective-permute-done | bytes 688160 | tf_op jit(solution)/shard_map/ppermute | solution.py:31
  83.0 3.9 %collective-permute-done.10.refs_9_ = bf16[48,7168]{1,0:T(8,128)(2,1)S(1)} collective-permute-done((bf16[48,7168]{1,0:T(8,128)(2,1)S(1)}, bf16[48,7168]{1,0:T(8,128)(2,1)S(1)}, u32[]{:S(2)}, u32[]{:S(2)}) %collective-permute-start.10) | collective-permute-done | bytes 688160 | tf_op jit(solution)/shard_map/ppermute | solution.py:31
  87.8 2.4 %collective-permute-start.13 = (bf16[16,7168]{1,0:T(8,128)(2,1)S(1)}, bf16[16,7168]{1,0:T(8,128)(2,1)}, u32[]{:S(2)}, u32[]{:S(2)}) collective-permute-start(bf16[16,7168]{1,0:T(8,128)(2,1)S(1)} %slice.448), channel_id=1, source_target_pairs={{0,6},{1,7},{2,0},{3,1},{4,2},{5,3},{6,4},{7,5},{8,14},{9,15},{10,... | collective-permute-start | bytes 688136 | tf_op jit(solution)/shard_map/ppermute | solution.py:31
  90.2 5.3 %collective-permute-start.4 = (bf16[128,7168]{1,0:T(8,128)(2,1)}, bf16[128,7168]{1,0:T(8,128)(2,1)}, u32[]{:S(2)}, u32[]{:S(2)}) collective-permute-start(bf16[128,7168]{1,0:T(8,128)(2,1)} %bitcast.166), channel_id=1, source_target_pairs={{32,0},{33,1},{34,2},{35,3},{36,4},{37,5},{38,6},{39,7},{40,8},{41... | collective-permute-start | bytes 5505032 | tf_op jit(solution)/shard_map/ppermute | solution.py:38
  95.5 1.9 collective-permute-start.5
  97.6 2.9 %collective-permute-start.33 = (bf16[48,7168]{1,0:T(8,128)(2,1)S(1)}, bf16[48,7168]{1,0:T(8,128)(2,1)}, u32[]{:S(2)}, u32[]{:S(2)}) collective-permute-start(bf16[48,7168]{1,0:T(8,128)(2,1)S(1)} %get-tuple-element.81), channel_id=1, source_target_pairs={{0,6},{1,7},{2,0},{3,1},{4,2},{5,3},{6,4},{7,5},{8,14},{9,15},{10,... | collective-permute-start | bytes 2064392 | tf_op jit(solution)/shard_map/ppermute | solution.py:31
  100.5 14.9 %shard_map.95 = bf16[256,7296]{1,0:T(8,128)(2,1)} custom-call(s32[1]{0:T(128)} %bitcast.13.piece_ref, bf16[32,7168]{1,0:T(8,128)(2,1)} %copy-done.8, bf16[32,7168]{1,0:T(8,128)(2,1)} %collective-permute-done.3.refs_1_, bf16[64,7168]{1,0:T(8,128)(2,1)} %copy-done.7, bf16[32,7168]{1,0:T(8,128)(2,1)} %copy-done.10, ...), custom_call_target="tpu_custom_call" | custom-call | flops 18790481920 | bytes 22020096 | tf_op jit(solution)/shard_map/pallas_call | solution.py:270
  115.3 2.5 %slice_bitcast_fusion.20 = (bf16[16,7296]{1,0:T(8,128)(2,1)S(1)}, bf16[16,7296]{1,0:T(8,128)(2,1)S(1)}, bf16[16,7296]{1,0:T(8,128)(2,1)}, bf16[16,7296]{1,0:T(8,...) fusion(bf16[2,8,16,7296]{3,2,1,0:T(8,128)(2,1)} %bitcast.162), kind=kLoop, calls=%fused_computation.99 | loop fusion | bytes 3735552 | tf_op jit(solution)/shard_map/squeeze | solution.py:360
  117.8 1.0 slice.499
  118.9 2.7 %collective-permute-start.36 = (bf16[16,7168]{1,0:T(8,128)(2,1)S(1)}, bf16[16,7168]{1,0:T(8,128)(2,1)S(1)}, u32[]{:S(2)}, u32[]{:S(2)}) collective-permute-start(bf16[16,7168]{1,0:T(8,128)(2,1)S(1)} %slice.500), channel_id=1, source_target_pairs={{0,6},{1,7},{2,0},{3,1},{4,2},{5,3},{6,4},{7,5},{8,14},{9,15},{10,... | collective-permute-start | bytes 688136 | tf_op jit(solution)/shard_map/ppermute | solution.py:31
  121.5 1.0 pad_maximum_fusion.8
  123.0 2.7 %collective-permute-start.16 = (bf16[16,7296]{1,0:T(8,128)(2,1)}, bf16[16,7296]{1,0:T(8,128)(2,1)S(1)}, u32[]{:S(2)}, u32[]{:S(2)}) collective-permute-start(bf16[16,7296]{1,0:T(8,128)(2,1)} %get-tuple-element.65), channel_id=1, source_target_pairs={{0,6},{1,7},{2,0},{3,1},{4,2},{5,3},{6,4},{7,5},{8,14},{9,15},{10,... | collective-permute-start | bytes 700424 | tf_op jit(solution)/shard_map/ppermute | solution.py:31
  125.7 1.5 collective-permute-done.35.refs_10_
  128.6 14.8 %shard_map.97 = bf16[256,7296]{1,0:T(8,128)(2,1)} custom-call(s32[1]{0:T(128)} %bitcast.13.piece_ref, bf16[32,7168]{1,0:T(8,128)(2,1)} %copy-done.27, bf16[32,7168]{1,0:T(8,128)(2,1)} %copy-done.18, bf16[64,7168]{1,0:T(8,128)(2,1)} %copy-done.6, bf16[32,7168]{1,0:T(8,128)(2,1)} %copy-done.9, bf16[32,7168]{1,0:T(8,128)(2,1)} %copy-done.17, ...), custom_call_target="tpu_custom_call" | custom-call | flops 18790481920 | bytes 22020096 | tf_op jit(solution)/shard_map/pallas_call | solution.py:270
  143.4 1.8 slice_bitcast_fusion.4
  145.8 2.7 %collective-permute-start.39 = (bf16[16,7296]{1,0:T(8,128)(2,1)S(1)}, bf16[16,7296]{1,0:T(8,128)(2,1)S(1)}, u32[]{:S(2)}, u32[]{:S(2)}) collective-permute-start(bf16[16,7296]{1,0:T(8,128)(2,1)S(1)} %get-tuple-element.87), channel_id=1, source_target_pairs={{0,6},{1,7},{2,0},{3,1},{4,2},{5,3},{6,4},{7,5},{8,14},{9,15},{10,... | collective-permute-start | bytes 700424 | tf_op jit(solution)/shard_map/ppermute | solution.py:31
  148.4 1.5 fusion.26
  150.1 2.7 %collective-permute-start.18 = (bf16[40,7296]{1,0:T(8,128)(2,1)S(1)}, bf16[40,7296]{1,0:T(8,128)(2,1)S(1)}, u32[]{:S(2)}, u32[]{:S(2)}) collective-permute-start(bf16[40,7296]{1,0:T(8,128)(2,1)S(1)} %pad_maximum_fusion.17), channel_id=1, source_target_pairs={{0,6},{1,7},{2,0},{3,1},{4,2},{5,3},{6,4},{7,5},{8,14},{9,15},{10,... | collective-permute-start | bytes 1751048 | tf_op jit(solution)/shard_map/ppermute | solution.py:31
  153.5 13.7 %collective-permute-done.37 = bf16[64,7296]{1,0:T(8,128)(2,1)S(1)} collective-permute-done((bf16[64,7296]{1,0:T(8,128)(2,1)S(1)}, bf16[64,7296]{1,0:T(8,128)(2,1)S(1)}, u32[]{:S(2)}, u32[]{:S(2)}) %collective-permute-start.37) | collective-permute-done | bytes 933920 | tf_op jit(solution)/shard_map/ppermute | solution.py:31
  167.2 1.6 fusion.15
  169.3 2.7 %collective-permute-start.20 = (bf16[16,7296]{1,0:T(8,128)(2,1)S(1)}, bf16[16,7296]{1,0:T(8,128)(2,1)S(1)}, u32[]{:S(2)}, u32[]{:S(2)}) collective-permute-start(bf16[16,7296]{1,0:T(8,128)(2,1)S(1)} %pad_maximum_fusion.27), channel_id=1, source_target_pairs={{0,6},{1,7},{2,0},{3,1},{4,2},{5,3},{6,4},{7,5},{8,14},{9,15},{10,... | collective-permute-start | bytes 700424 | tf_op jit(solution)/shard_map/ppermute | solution.py:31
  172.5 2.7 %collective-permute-start.41 = (bf16[40,7296]{1,0:T(8,128)(2,1)S(1)}, bf16[40,7296]{1,0:T(8,128)(2,1)S(1)}, u32[]{:S(2)}, u32[]{:S(2)}) collective-permute-start(bf16[40,7296]{1,0:T(8,128)(2,1)S(1)} %pad_maximum_fusion.19), channel_id=1, source_target_pairs={{0,6},{1,7},{2,0},{3,1},{4,2},{5,3},{6,4},{7,5},{8,14},{9,15},{10,... | collective-permute-start | bytes 1751048 | tf_op jit(solution)/shard_map/ppermute | solution.py:31
  175.2 1.3 collective-permute-done.19
  176.4 0.9 collective-permute-done.21
  177.3 1.2 fusion.23
  178.6 4.9 %collective-permute-start.22 = (bf16[16,7168]{1,0:T(8,128)(2,1)S(1)}, bf16[16,7168]{1,0:T(8,128)(2,1)S(1)}, u32[]{:S(2)}, u32[]{:S(2)}) collective-permute-start(bf16[16,7168]{1,0:T(8,128)(2,1)S(1)} %slice.478), channel_id=1, source_target_pairs={{32,0},{33,1},{34,2},{35,3},{36,4},{37,5},{38,6},{39,7},{40,8},{41... | collective-permute-start | bytes 688136 | tf_op jit(solution)/shard_map/ppermute | solution.py:38
  183.5 2.4 %collective-permute-start.23 = (bf16[16,7168]{1,0:T(8,128)(2,1)S(1)}, bf16[16,7168]{1,0:T(8,128)(2,1)S(1)}, u32[]{:S(2)}, u32[]{:S(2)}) collective-permute-start(bf16[16,7168]{1,0:T(8,128)(2,1)S(1)} %slice.483), channel_id=1, source_target_pairs={{32,24},{33,25},{34,26},{35,27},{36,28},{37,29},{38,30},{39,31},{4... | collective-permute-start | bytes 688136 | tf_op jit(solution)/shard_map/ppermute | solution.py:38
  186.7 1.5 collective-permute-done.41
  188.9 1.0 fusion.14
  191.2 2.2 collective-permute-start.43
  194.1 1.3 collective-permute-done.23.refs_1_
  196.1 7.0 %shard_map.96 = f32[128,7168]{1,0:T(8,128)} custom-call(bf16[128,7168]{1,0:T(8,128)(2,1)} %collective-permute-done.4.base_ref, f32[128,32]{1,0:T(8,128)} %bitcast.167, bf16[16,7168]{1,0:T(8,128)(2,1)} %copy-done.29, bf16[16,7168]{1,0:T(8,128)(2,1)} %copy-done.31), custom_call_target="tpu_custom_call" | custom-call | flops 24999999488 | bytes 7340032 | tf_op jit(solution)/shard_map/pallas_call | solution.py:305
  203.1 1.6 fusion.12
  204.8 1.1 collective-permute-start.48
  205.8 2.0 collective-permute-start.49
  207.8 4.2 %collective-permute-start.45 = (bf16[16,7168]{1,0:T(8,128)(2,1)S(1)}, bf16[16,7168]{1,0:T(8,128)(2,1)S(1)}, u32[]{:S(2)}, u32[]{:S(2)}) collective-permute-start(bf16[16,7168]{1,0:T(8,128)(2,1)S(1)} %slice.536), channel_id=1, source_target_pairs={{32,16},{33,17},{34,18},{35,19},{36,20},{37,21},{38,22},{39,23},{4... | collective-permute-start | bytes 688136 | tf_op jit(solution)/shard_map/ppermute | solution.py:38
  212.1 1.9 collective-permute-start.46
  214.9 6.1 %collective-permute-done.45 = bf16[16,7168]{1,0:T(8,128)(2,1)S(1)} collective-permute-done((bf16[16,7168]{1,0:T(8,128)(2,1)S(1)}, bf16[16,7168]{1,0:T(8,128)(2,1)S(1)}, u32[]{:S(2)}, u32[]{:S(2)}) %collective-permute-start.45) | collective-permute-done | bytes 229408 | tf_op jit(solution)/shard_map/ppermute | solution.py:38
  221.0 5.4 %collective-permute-done.46 = bf16[16,7168]{1,0:T(8,128)(2,1)S(1)} collective-permute-done((bf16[16,7168]{1,0:T(8,128)(2,1)S(1)}, bf16[16,7168]{1,0:T(8,128)(2,1)S(1)}, u32[]{:S(2)}, u32[]{:S(2)}) %collective-permute-start.46) | collective-permute-done | bytes 229408 | tf_op jit(solution)/shard_map/ppermute | solution.py:38
  227.1 1.3 copy-done.3
  228.5 2.1 fusion.3
  (192 shorter events, 18.5 us)
Async XLA Ops:
  4.1 8.4 %copy-start.24 = (s32[1,128,8]{1,2,0:T(8,128)S(1)}, s32[1,128,8]{1,2,0:T(8,128)}, u32[]{:S(2)}) copy-start(s32[1,128,8]{1,2,0:T(8,128)} %param.10) | copy-start | bytes 12292
  4.1 8.4 %copy-start.25 = (f32[1,128,8]{1,2,0:T(8,128)S(1)}, f32[1,128,8]{1,2,0:T(8,128)}, u32[]{:S(2)}) copy-start(f32[1,128,8]{1,2,0:T(8,128)} %param.11) | copy-start | bytes 12292
  4.2 12.6 %collective-permute-start.24 = (bf16[32,7168]{1,0:T(8,128)(2,1)S(1)}, bf16[32,7168]{1,0:T(8,128)(2,1)S(1)}, u32[]{:S(2)}, u32[]{:S(2)}) collective-permute-start(bf16[32,7168]{1,0:T(8,128)(2,1)S(1)} %pad_maximum_fusion.23), channel_id=1, source_target_pairs={{0,24},{1,25},{2,26},{3,27},{4,28},{5,29},{6,30},{7,31},{8,0},{9,1... | collective-permute-start | bytes 1376264 | tf_op jit(solution)/shard_map/ppermute | solution.py:31
  7.6 18.6 %copy-start.8 = (bf16[32,7168]{1,0:T(8,128)(2,1)}, bf16[32,7168]{1,0:T(8,128)(2,1)S(1)}, u32[]{:S(2)}) copy-start(bf16[32,7168]{1,0:T(8,128)(2,1)S(1)} %get-tuple-element.51.refs_0_) | copy-start | bytes 1376260
  7.6 12.5 %collective-permute-start.1 = (bf16[32,7168]{1,0:T(8,128)(2,1)S(1)}, bf16[32,7168]{1,0:T(8,128)(2,1)S(1)}, u32[]{:S(2)}, u32[]{:S(2)}) collective-permute-start(bf16[32,7168]{1,0:T(8,128)(2,1)S(1)} %get-tuple-element.51.refs_0_), channel_id=1, source_target_pairs={{0,2},{1,3},{2,4},{3,5},{4,6},{5,7},{6,0},{7,1},{8,10},{9,11},{10,... | collective-permute-start | bytes 1376264 | tf_op jit(solution)/shard_map/ppermute | solution.py:31
  9.0 12.8 %collective-permute-start.2 = (bf16[32,7168]{1,0:T(8,128)(2,1)S(1)}, bf16[32,7168]{1,0:T(8,128)(2,1)}, u32[]{:S(2)}, u32[]{:S(2)}) collective-permute-start(bf16[32,7168]{1,0:T(8,128)(2,1)S(1)} %get-tuple-element.51.refs_0_), channel_id=1, source_target_pairs={{0,1},{1,0},{2,3},{3,2},{4,5},{5,4},{6,7},{7,6},{8,9},{9,8},{10,11... | collective-permute-start | bytes 1376264 | tf_op jit(solution)/shard_map/ppermute | solution.py:31
  10.6 13.7 %collective-permute-start.3 = (bf16[32,7168]{1,0:T(8,128)(2,1)S(1)}, bf16[32,7168]{1,0:T(8,128)(2,1)}, u32[]{:S(2)}, u32[]{:S(2)}) collective-permute-start(bf16[32,7168]{1,0:T(8,128)(2,1)S(1)} %get-tuple-element.51.refs_0_), channel_id=1, source_target_pairs={{0,6},{1,7},{2,0},{3,1},{4,2},{5,3},{6,4},{7,5},{8,14},{9,15},{10,... | collective-permute-start | bytes 1376264 | tf_op jit(solution)/shard_map/ppermute | solution.py:31
  12.2 13.7 %collective-permute-start = (bf16[32,7168]{1,0:T(8,128)(2,1)S(1)}, bf16[32,7168]{1,0:T(8,128)(2,1)S(1)}, u32[]{:S(2)}, u32[]{:S(2)}) collective-permute-start(bf16[32,7168]{1,0:T(8,128)(2,1)S(1)} %pad_maximum_fusion.20), channel_id=1, source_target_pairs={{0,8},{1,9},{2,10},{3,11},{4,12},{5,13},{6,14},{7,15},{8,16},{9,17... | collective-permute-start | bytes 1376264 | tf_op jit(solution)/shard_map/ppermute | solution.py:31
  16.8 9.5 %copy-start.27 = (bf16[32,7168]{1,0:T(8,128)(2,1)}, bf16[32,7168]{1,0:T(8,128)(2,1)S(1)}, u32[]{:S(2)}) copy-start(bf16[32,7168]{1,0:T(8,128)(2,1)S(1)} %collective-permute-done.24.refs_0_) | copy-start | bytes 1376260
  16.8 13.4 %collective-permute-start.27 = (bf16[32,7168]{1,0:T(8,128)(2,1)S(1)}, bf16[32,7168]{1,0:T(8,128)(2,1)S(1)}, u32[]{:S(2)}, u32[]{:S(2)}) collective-permute-start(bf16[32,7168]{1,0:T(8,128)(2,1)S(1)} %collective-permute-done.24.refs_0_), channel_id=1, source_target_pairs={{0,2},{1,3},{2,4},{3,5},{4,6},{5,7},{6,0},{7,1},{8,10},{9,11},{10,... | collective-permute-start | bytes 1376264 | tf_op jit(solution)/shard_map/ppermute | solution.py:31
  20.1 11.4 %collective-permute-start.28 = (bf16[32,7168]{1,0:T(8,128)(2,1)S(1)}, bf16[32,7168]{1,0:T(8,128)(2,1)S(1)}, u32[]{:S(2)}, u32[]{:S(2)}) collective-permute-start(bf16[32,7168]{1,0:T(8,128)(2,1)S(1)} %collective-permute-done.24.refs_0_), channel_id=1, source_target_pairs={{0,1},{1,0},{2,3},{3,2},{4,5},{5,4},{6,7},{7,6},{8,9},{9,8},{10,11... | collective-permute-start | bytes 1376264 | tf_op jit(solution)/shard_map/ppermute | solution.py:31
  21.8 11.5 %collective-permute-start.25 = (bf16[32,7168]{1,0:T(8,128)(2,1)S(1)}, bf16[32,7168]{1,0:T(8,128)(2,1)S(1)}, u32[]{:S(2)}, u32[]{:S(2)}) collective-permute-start(bf16[32,7168]{1,0:T(8,128)(2,1)S(1)} %collective-permute-done.24.refs_0_), channel_id=1, source_target_pairs={{0,6},{1,7},{2,0},{3,1},{4,2},{5,3},{6,4},{7,5},{8,14},{9,15},{10,... | collective-permute-start | bytes 1376264 | tf_op jit(solution)/shard_map/ppermute | solution.py:31
  24.3 10.6 %collective-permute-start.26 = (bf16[32,7168]{1,0:T(8,128)(2,1)S(1)}, bf16[32,7168]{1,0:T(8,128)(2,1)S(1)}, u32[]{:S(2)}, u32[]{:S(2)}) collective-permute-start(bf16[32,7168]{1,0:T(8,128)(2,1)S(1)} %get-tuple-element.74), channel_id=1, source_target_pairs={{0,16},{1,17},{2,18},{3,19},{4,20},{5,21},{6,22},{7,23},{8,24},{9,... | collective-permute-start | bytes 1376264 | tf_op jit(solution)/shard_map/ppermute | solution.py:31
  26.7 25.9 %collective-permute-start.6 = (bf16[64,7168]{1,0:T(8,128)(2,1)S(1)}, bf16[64,7168]{1,0:T(8,128)(2,1)S(1)}, u32[]{:S(2)}, u32[]{:S(2)}) collective-permute-start(bf16[64,7168]{1,0:T(8,128)(2,1)S(1)} %get-tuple-element.55), channel_id=1, source_target_pairs={{0,2},{1,3},{2,4},{3,5},{4,6},{5,7},{6,0},{7,1},{8,10},{9,11},{10,... | collective-permute-start | bytes 2752520 | tf_op jit(solution)/shard_map/ppermute | solution.py:31
  30.1 4.8 %copy-start.9 = (bf16[32,7168]{1,0:T(8,128)(2,1)}, bf16[32,7168]{1,0:T(8,128)(2,1)S(1)}, u32[]{:S(2)}) copy-start(bf16[32,7168]{1,0:T(8,128)(2,1)S(1)} %collective-permute-done.27.refs_3_) | copy-start | bytes 1376260
  30.1 22.4 %collective-permute-start.7 = (bf16[64,7168]{1,0:T(8,128)(2,1)S(1)}, bf16[64,7168]{1,0:T(8,128)(2,1)S(1)}, u32[]{:S(2)}, u32[]{:S(2)}) collective-permute-start(bf16[64,7168]{1,0:T(8,128)(2,1)S(1)} %get-tuple-element.56), channel_id=1, source_target_pairs={{0,6},{1,7},{2,0},{3,1},{4,2},{5,3},{6,4},{7,5},{8,14},{9,15},{10,... | collective-permute-start | bytes 2752520 | tf_op jit(solution)/shard_map/ppermute | solution.py:31
  31.6 3.3 %copy-start.17 = (bf16[32,7168]{1,0:T(8,128)(2,1)}, bf16[32,7168]{1,0:T(8,128)(2,1)S(1)}, u32[]{:S(2)}) copy-start(bf16[32,7168]{1,0:T(8,128)(2,1)S(1)} %collective-permute-done.28.refs_4_) | copy-start | bytes 1376260
  31.6 21.1 %collective-permute-start.8 = (bf16[64,7168]{1,0:T(8,128)(2,1)S(1)}, bf16[64,7168]{1,0:T(8,128)(2,1)S(1)}, u32[]{:S(2)}, u32[]{:S(2)}) collective-permute-start(bf16[64,7168]{1,0:T(8,128)(2,1)S(1)} %get-tuple-element.57), channel_id=1, source_target_pairs={{0,1},{1,0},{2,3},{3,2},{4,5},{5,4},{6,7},{7,6},{8,9},{9,8},{10,11... | collective-permute-start | bytes 2752520 | tf_op jit(solution)/shard_map/ppermute | solution.py:31
  35.7 36.6 %collective-permute-start.29 = (bf16[64,7168]{1,0:T(8,128)(2,1)S(1)}, bf16[64,7168]{1,0:T(8,128)(2,1)S(1)}, u32[]{:S(2)}, u32[]{:S(2)}) collective-permute-start(bf16[64,7168]{1,0:T(8,128)(2,1)S(1)} %get-tuple-element.77), channel_id=1, source_target_pairs={{0,2},{1,3},{2,4},{3,5},{4,6},{5,7},{6,0},{7,1},{8,10},{9,11},{10,... | collective-permute-start | bytes 2752520 | tf_op jit(solution)/shard_map/ppermute | solution.py:31
  35.7 36.5 %collective-permute-start.30 = (bf16[64,7168]{1,0:T(8,128)(2,1)S(1)}, bf16[64,7168]{1,0:T(8,128)(2,1)S(1)}, u32[]{:S(2)}, u32[]{:S(2)}) collective-permute-start(bf16[64,7168]{1,0:T(8,128)(2,1)S(1)} %get-tuple-element.78), channel_id=1, source_target_pairs={{0,6},{1,7},{2,0},{3,1},{4,2},{5,3},{6,4},{7,5},{8,14},{9,15},{10,... | collective-permute-start | bytes 2752520 | tf_op jit(solution)/shard_map/ppermute | solution.py:31
  52.6 19.8 %collective-permute-start.31 = (bf16[64,7168]{1,0:T(8,128)(2,1)S(1)}, bf16[64,7168]{1,0:T(8,128)(2,1)S(1)}, u32[]{:S(2)}, u32[]{:S(2)}) collective-permute-start(bf16[64,7168]{1,0:T(8,128)(2,1)S(1)} %get-tuple-element.79), channel_id=1, source_target_pairs={{0,1},{1,0},{2,3},{3,2},{4,5},{5,4},{6,7},{7,6},{8,9},{9,8},{10,11... | collective-permute-start | bytes 2752520 | tf_op jit(solution)/shard_map/ppermute | solution.py:31
  54.1 28.9 %collective-permute-start.9 = (bf16[48,7168]{1,0:T(8,128)(2,1)S(1)}, bf16[48,7168]{1,0:T(8,128)(2,1)S(1)}, u32[]{:S(2)}, u32[]{:S(2)}) collective-permute-start(bf16[48,7168]{1,0:T(8,128)(2,1)S(1)} %get-tuple-element.58), channel_id=1, source_target_pairs={{0,2},{1,3},{2,4},{3,5},{4,6},{5,7},{6,0},{7,1},{8,10},{9,11},{10,... | collective-permute-start | bytes 2064392 | tf_op jit(solution)/shard_map/ppermute | solution.py:31
  54.1 32.9 %collective-permute-start.10 = (bf16[48,7168]{1,0:T(8,128)(2,1)S(1)}, bf16[48,7168]{1,0:T(8,128)(2,1)S(1)}, u32[]{:S(2)}, u32[]{:S(2)}) collective-permute-start(bf16[48,7168]{1,0:T(8,128)(2,1)S(1)} %get-tuple-element.59), channel_id=1, source_target_pairs={{0,6},{1,7},{2,0},{3,1},{4,2},{5,3},{6,4},{7,5},{8,14},{9,15},{10,... | collective-permute-start | bytes 2064392 | tf_op jit(solution)/shard_map/ppermute | solution.py:31
  72.2 8.4 %collective-permute-start.11 = (bf16[32,7168]{1,0:T(8,128)(2,1)S(1)}, bf16[32,7168]{1,0:T(8,128)(2,1)S(1)}, u32[]{:S(2)}, u32[]{:S(2)}) collective-permute-start(bf16[32,7168]{1,0:T(8,128)(2,1)S(1)} %pad_maximum_fusion.22), channel_id=1, source_target_pairs={{0,1},{1,0},{2,3},{3,2},{4,5},{5,4},{6,7},{7,6},{8,9},{9,8},{10,11... | collective-permute-start | bytes 1376264 | tf_op jit(solution)/shard_map/ppermute | solution.py:31
  73.7 23.7 %collective-permute-start.34 = (bf16[32,7168]{1,0:T(8,128)(2,1)S(1)}, bf16[32,7168]{1,0:T(8,128)(2,1)S(1)}, u32[]{:S(2)}, u32[]{:S(2)}) collective-permute-start(bf16[32,7168]{1,0:T(8,128)(2,1)S(1)} %pad_maximum_fusion.25), channel_id=1, source_target_pairs={{0,1},{1,0},{2,3},{3,2},{4,5},{5,4},{6,7},{7,6},{8,9},{9,8},{10,11... | collective-permute-start | bytes 1376264 | tf_op jit(solution)/shard_map/ppermute | solution.py:31
  80.6 19.9 %copy-start.20 = (bf16[32,7168]{1,0:T(8,128)(2,1)}, bf16[32,7168]{1,0:T(8,128)(2,1)S(1)}, u32[]{:S(2)}) copy-start(bf16[32,7168]{1,0:T(8,128)(2,1)S(1)} %collective-permute-done.11.refs_11_) | copy-start | bytes 1376260
  83.0 3.9 %copy-start.21 = (bf16[48,7168]{1,0:T(8,128)(2,1)}, bf16[48,7168]{1,0:T(8,128)(2,1)S(1)}, u32[]{:S(2)}) copy-start(bf16[48,7168]{1,0:T(8,128)(2,1)S(1)} %collective-permute-done.9.refs_6_) | copy-start | bytes 2064388
  87.0 10.6 %collective-permute-start.12 = (bf16[16,7168]{1,0:T(8,128)(2,1)S(1)}, bf16[16,7168]{1,0:T(8,128)(2,1)}, u32[]{:S(2)}, u32[]{:S(2)}) collective-permute-start(bf16[16,7168]{1,0:T(8,128)(2,1)S(1)} %slice.447), channel_id=1, source_target_pairs={{0,2},{1,3},{2,4},{3,5},{4,6},{5,7},{6,0},{7,1},{8,10},{9,11},{10,... | collective-permute-start | bytes 688136 | tf_op jit(solution)/shard_map/ppermute | solution.py:31
  87.8 12.7 %collective-permute-start.13 = (bf16[16,7168]{1,0:T(8,128)(2,1)S(1)}, bf16[16,7168]{1,0:T(8,128)(2,1)}, u32[]{:S(2)}, u32[]{:S(2)}) collective-permute-start(bf16[16,7168]{1,0:T(8,128)(2,1)S(1)} %slice.448), channel_id=1, source_target_pairs={{0,6},{1,7},{2,0},{3,1},{4,2},{5,3},{6,4},{7,5},{8,14},{9,15},{10,... | collective-permute-start | bytes 688136 | tf_op jit(solution)/shard_map/ppermute | solution.py:31
  90.2 32.3 %collective-permute-start.4 = (bf16[128,7168]{1,0:T(8,128)(2,1)}, bf16[128,7168]{1,0:T(8,128)(2,1)}, u32[]{:S(2)}, u32[]{:S(2)}) collective-permute-start(bf16[128,7168]{1,0:T(8,128)(2,1)} %bitcast.166), channel_id=1, source_target_pairs={{32,0},{33,1},{34,2},{35,3},{36,4},{37,5},{38,6},{39,7},{40,8},{41... | collective-permute-start | bytes 5505032 | tf_op jit(solution)/shard_map/ppermute | solution.py:38
  95.5 27.0 %collective-permute-start.5 = (f32[128,64]{1,0:T(8,128)S(1)}, f32[128,64]{1,0:T(8,128)S(1)}, u32[]{:S(2)}, u32[]{:S(2)}) collective-permute-start(f32[128,64]{1,0:T(8,128)S(1)} %and_select_fusion), channel_id=1, source_target_pairs={{32,0},{33,1},{34,2},{35,3},{36,4},{37,5},{38,6},{39,7},{40,8},{41... | collective-permute-start | bytes 98312 | tf_op jit(solution)/shard_map/ppermute | solution.py:38
  97.4 17.9 %copy-start.19 = (bf16[32,7168]{1,0:T(8,128)(2,1)}, bf16[32,7168]{1,0:T(8,128)(2,1)S(1)}, u32[]{:S(2)}) copy-start(bf16[32,7168]{1,0:T(8,128)(2,1)S(1)} %collective-permute-done.34.refs_11_) | copy-start | bytes 1376260
  97.5 20.4 %collective-permute-start.32 = (bf16[48,7168]{1,0:T(8,128)(2,1)S(1)}, bf16[48,7168]{1,0:T(8,128)(2,1)}, u32[]{:S(2)}, u32[]{:S(2)}) collective-permute-start(bf16[48,7168]{1,0:T(8,128)(2,1)S(1)} %get-tuple-element.80), channel_id=1, source_target_pairs={{0,2},{1,3},{2,4},{3,5},{4,6},{5,7},{6,0},{7,1},{8,10},{9,11},{10,... | collective-permute-start | bytes 2064392 | tf_op jit(solution)/shard_map/ppermute | solution.py:31
  97.6 21.2 %collective-permute-start.33 = (bf16[48,7168]{1,0:T(8,128)(2,1)S(1)}, bf16[48,7168]{1,0:T(8,128)(2,1)}, u32[]{:S(2)}, u32[]{:S(2)}) collective-permute-start(bf16[48,7168]{1,0:T(8,128)(2,1)S(1)} %get-tuple-element.81), channel_id=1, source_target_pairs={{0,6},{1,7},{2,0},{3,1},{4,2},{5,3},{6,4},{7,5},{8,14},{9,15},{10,... | collective-permute-start | bytes 2064392 | tf_op jit(solution)/shard_map/ppermute | solution.py:31
  118.8 8.4 %collective-permute-start.35 = (bf16[16,7168]{1,0:T(8,128)(2,1)S(1)}, bf16[16,7168]{1,0:T(8,128)(2,1)S(1)}, u32[]{:S(2)}, u32[]{:S(2)}) collective-permute-start(bf16[16,7168]{1,0:T(8,128)(2,1)S(1)} %slice.499), channel_id=1, source_target_pairs={{0,2},{1,3},{2,4},{3,5},{4,6},{5,7},{6,0},{7,1},{8,10},{9,11},{10,... | collective-permute-start | bytes 688136 | tf_op jit(solution)/shard_map/ppermute | solution.py:31
  118.9 8.3 %collective-permute-start.36 = (bf16[16,7168]{1,0:T(8,128)(2,1)S(1)}, bf16[16,7168]{1,0:T(8,128)(2,1)S(1)}, u32[]{:S(2)}, u32[]{:S(2)}) collective-permute-start(bf16[16,7168]{1,0:T(8,128)(2,1)S(1)} %slice.500), channel_id=1, source_target_pairs={{0,6},{1,7},{2,0},{3,1},{4,2},{5,3},{6,4},{7,5},{8,14},{9,15},{10,... | collective-permute-start | bytes 688136 | tf_op jit(solution)/shard_map/ppermute | solution.py:31
  122.5 20.8 %copy-start.13 = (f32[128,64]{1,0:T(8,128)}, f32[128,64]{1,0:T(8,128)S(1)}, u32[]{:S(2)}) copy-start(f32[128,64]{1,0:T(8,128)S(1)} %collective-permute-done.5) | copy-start | bytes 98308
  122.5 25.9 %collective-permute-start.14 = (bf16[64,7296]{1,0:T(8,128)(2,1)}, bf16[64,7296]{1,0:T(8,128)(2,1)}, u32[]{:S(2)}, u32[]{:S(2)}) collective-permute-start(bf16[64,7296]{1,0:T(8,128)(2,1)} %pad_maximum_fusion.8), channel_id=1, source_target_pairs={{0,1},{1,0},{2,3},{3,2},{4,5},{5,4},{6,7},{7,6},{8,9},{9,8},{10,11... | collective-permute-start | bytes 2801672 | tf_op jit(solution)/shard_map/ppermute | solution.py:31
  123.0 22.7 %collective-permute-start.15 = (bf16[16,7296]{1,0:T(8,128)(2,1)}, bf16[16,7296]{1,0:T(8,128)(2,1)S(1)}, u32[]{:S(2)}, u32[]{:S(2)}) collective-permute-start(bf16[16,7296]{1,0:T(8,128)(2,1)} %get-tuple-element.64), channel_id=1, source_target_pairs={{0,2},{1,3},{2,4},{3,5},{4,6},{5,7},{6,0},{7,1},{8,10},{9,11},{10,... | collective-permute-start | bytes 700424 | tf_op jit(solution)/shard_map/ppermute | solution.py:31
  123.0 25.4 %collective-permute-start.16 = (bf16[16,7296]{1,0:T(8,128)(2,1)}, bf16[16,7296]{1,0:T(8,128)(2,1)S(1)}, u32[]{:S(2)}, u32[]{:S(2)}) collective-permute-start(bf16[16,7296]{1,0:T(8,128)(2,1)} %get-tuple-element.65), channel_id=1, source_target_pairs={{0,6},{1,7},{2,0},{3,1},{4,2},{5,3},{6,4},{7,5},{8,14},{9,15},{10,... | collective-permute-start | bytes 700424 | tf_op jit(solution)/shard_map/ppermute | solution.py:31
  143.4 5.1 %copy-start.2 = (bf16[256,7296]{1,0:T(8,128)(2,1)S(1)}, bf16[256,7296]{1,0:T(8,128)(2,1)}, u32[]{:S(2)}) copy-start(bf16[256,7296]{1,0:T(8,128)(2,1)} %shard_map.95) | copy-start | bytes 11206660
  145.3 22.0 %collective-permute-start.37 = (bf16[64,7296]{1,0:T(8,128)(2,1)S(1)}, bf16[64,7296]{1,0:T(8,128)(2,1)S(1)}, u32[]{:S(2)}, u32[]{:S(2)}) collective-permute-start(bf16[64,7296]{1,0:T(8,128)(2,1)S(1)} %pad_maximum_fusion.9), channel_id=1, source_target_pairs={{0,1},{1,0},{2,3},{3,2},{4,5},{5,4},{6,7},{7,6},{8,9},{9,8},{10,11... | collective-permute-start | bytes 2801672 | tf_op jit(solution)/shard_map/ppermute | solution.py:31
  145.7 7.8 %collective-permute-start.38 = (bf16[16,7296]{1,0:T(8,128)(2,1)S(1)}, bf16[16,7296]{1,0:T(8,128)(2,1)S(1)}, u32[]{:S(2)}, u32[]{:S(2)}) collective-permute-start(bf16[16,7296]{1,0:T(8,128)(2,1)S(1)} %get-tuple-element.86), channel_id=1, source_target_pairs={{0,2},{1,3},{2,4},{3,5},{4,6},{5,7},{6,0},{7,1},{8,10},{9,11},{10,... | collective-permute-start | bytes 700424 | tf_op jit(solution)/shard_map/ppermute | solution.py:31
  145.8 7.8 %collective-permute-start.39 = (bf16[16,7296]{1,0:T(8,128)(2,1)S(1)}, bf16[16,7296]{1,0:T(8,128)(2,1)S(1)}, u32[]{:S(2)}, u32[]{:S(2)}) collective-permute-start(bf16[16,7296]{1,0:T(8,128)(2,1)S(1)} %get-tuple-element.87), channel_id=1, source_target_pairs={{0,6},{1,7},{2,0},{3,1},{4,2},{5,3},{6,4},{7,5},{8,14},{9,15},{10,... | collective-permute-start | bytes 700424 | tf_op jit(solution)/shard_map/ppermute | solution.py:31
  150.0 19.0 %collective-permute-start.17 = (bf16[40,7296]{1,0:T(8,128)(2,1)S(1)}, bf16[40,7296]{1,0:T(8,128)(2,1)S(1)}, u32[]{:S(2)}, u32[]{:S(2)}) collective-permute-start(bf16[40,7296]{1,0:T(8,128)(2,1)S(1)} %pad_maximum_fusion.16), channel_id=1, source_target_pairs={{0,2},{1,3},{2,4},{3,5},{4,6},{5,7},{6,0},{7,1},{8,10},{9,11},{10,... | collective-permute-start | bytes 1751048 | tf_op jit(solution)/shard_map/ppermute | solution.py:31
  150.1 18.8 %collective-permute-start.18 = (bf16[40,7296]{1,0:T(8,128)(2,1)S(1)}, bf16[40,7296]{1,0:T(8,128)(2,1)S(1)}, u32[]{:S(2)}, u32[]{:S(2)}) collective-permute-start(bf16[40,7296]{1,0:T(8,128)(2,1)S(1)} %pad_maximum_fusion.17), channel_id=1, source_target_pairs={{0,6},{1,7},{2,0},{3,1},{4,2},{5,3},{6,4},{7,5},{8,14},{9,15},{10,... | collective-permute-start | bytes 1751048 | tf_op jit(solution)/shard_map/ppermute | solution.py:31
  169.2 7.2 %collective-permute-start.19 = (bf16[16,7296]{1,0:T(8,128)(2,1)S(1)}, bf16[16,7296]{1,0:T(8,128)(2,1)S(1)}, u32[]{:S(2)}, u32[]{:S(2)}) collective-permute-start(bf16[16,7296]{1,0:T(8,128)(2,1)S(1)} %pad_maximum_fusion.26), channel_id=1, source_target_pairs={{0,2},{1,3},{2,4},{3,5},{4,6},{5,7},{6,0},{7,1},{8,10},{9,11},{10,... | collective-permute-start | bytes 700424 | tf_op jit(solution)/shard_map/ppermute | solution.py:31
  169.3 7.2 %collective-permute-start.20 = (bf16[16,7296]{1,0:T(8,128)(2,1)S(1)}, bf16[16,7296]{1,0:T(8,128)(2,1)S(1)}, u32[]{:S(2)}, u32[]{:S(2)}) collective-permute-start(bf16[16,7296]{1,0:T(8,128)(2,1)S(1)} %pad_maximum_fusion.27), channel_id=1, source_target_pairs={{0,6},{1,7},{2,0},{3,1},{4,2},{5,3},{6,4},{7,5},{8,14},{9,15},{10,... | collective-permute-start | bytes 700424 | tf_op jit(solution)/shard_map/ppermute | solution.py:31
  171.9 5.4 %collective-permute-start.21 = (bf16[16,7296]{1,0:T(8,128)(2,1)S(1)}, bf16[16,7296]{1,0:T(8,128)(2,1)S(1)}, u32[]{:S(2)}, u32[]{:S(2)}) collective-permute-start(bf16[16,7296]{1,0:T(8,128)(2,1)S(1)} %fusion.25), channel_id=1, source_target_pairs={{0,1},{1,0},{2,3},{3,2},{4,5},{5,4},{6,7},{7,6},{8,9},{9,8},{10,11... | collective-permute-start | bytes 700424 | tf_op jit(solution)/shard_map/ppermute | solution.py:31
  172.4 16.6 %collective-permute-start.40 = (bf16[40,7296]{1,0:T(8,128)(2,1)S(1)}, bf16[40,7296]{1,0:T(8,128)(2,1)S(1)}, u32[]{:S(2)}, u32[]{:S(2)}) collective-permute-start(bf16[40,7296]{1,0:T(8,128)(2,1)S(1)} %pad_maximum_fusion.18), channel_id=1, source_target_pairs={{0,2},{1,3},{2,4},{3,5},{4,6},{5,7},{6,0},{7,1},{8,10},{9,11},{10,... | collective-permute-start | bytes 1751048 | tf_op jit(solution)/shard_map/ppermute | solution.py:31
  172.5 15.7 %collective-permute-start.41 = (bf16[40,7296]{1,0:T(8,128)(2,1)S(1)}, bf16[40,7296]{1,0:T(8,128)(2,1)S(1)}, u32[]{:S(2)}, u32[]{:S(2)}) collective-permute-start(bf16[40,7296]{1,0:T(8,128)(2,1)S(1)} %pad_maximum_fusion.19), channel_id=1, source_target_pairs={{0,6},{1,7},{2,0},{3,1},{4,2},{5,3},{6,4},{7,5},{8,14},{9,15},{10,... | collective-permute-start | bytes 1751048 | tf_op jit(solution)/shard_map/ppermute | solution.py:31
  178.6 14.9 %collective-permute-start.22 = (bf16[16,7168]{1,0:T(8,128)(2,1)S(1)}, bf16[16,7168]{1,0:T(8,128)(2,1)S(1)}, u32[]{:S(2)}, u32[]{:S(2)}) collective-permute-start(bf16[16,7168]{1,0:T(8,128)(2,1)S(1)} %slice.478), channel_id=1, source_target_pairs={{32,0},{33,1},{34,2},{35,3},{36,4},{37,5},{38,6},{39,7},{40,8},{41... | collective-permute-start | bytes 688136 | tf_op jit(solution)/shard_map/ppermute | solution.py:38
  183.5 11.9 %collective-permute-start.23 = (bf16[16,7168]{1,0:T(8,128)(2,1)S(1)}, bf16[16,7168]{1,0:T(8,128)(2,1)S(1)}, u32[]{:S(2)}, u32[]{:S(2)}) collective-permute-start(bf16[16,7168]{1,0:T(8,128)(2,1)S(1)} %slice.483), channel_id=1, source_target_pairs={{32,24},{33,25},{34,26},{35,27},{36,28},{37,29},{38,30},{39,31},{4... | collective-permute-start | bytes 688136 | tf_op jit(solution)/shard_map/ppermute | solution.py:38
  185.9 28.1 %collective-permute-start.47 = (bf16[16,128]{1,0:T(8,128)(2,1)S(1)}, bf16[16,128]{1,0:T(8,128)(2,1)S(1)}, u32[]{:S(2)}, u32[]{:S(2)}) collective-permute-start(bf16[16,128]{1,0:T(8,128)(2,1)S(1)} %slice.482), channel_id=1, source_target_pairs={{0,24},{1,25},{2,26},{3,27},{4,28},{5,29},{6,30},{7,31},{8,0},{9,1... | collective-permute-start | bytes 12296 | tf_op jit(solution)/shard_map/ppermute | solution.py:31
  190.7 12.4 %collective-permute-start.42 = (bf16[16,7296]{1,0:T(8,128)(2,1)}, bf16[16,7296]{1,0:T(8,128)(2,1)S(1)}, u32[]{:S(2)}, u32[]{:S(2)}) collective-permute-start(bf16[16,7296]{1,0:T(8,128)(2,1)} %pad_maximum_fusion.28), channel_id=1, source_target_pairs={{0,2},{1,3},{2,4},{3,5},{4,6},{5,7},{6,0},{7,1},{8,10},{9,11},{10,... | collective-permute-start | bytes 700424 | tf_op jit(solution)/shard_map/ppermute | solution.py:31
  191.2 11.9 %collective-permute-start.43 = (bf16[16,7296]{1,0:T(8,128)(2,1)S(1)}, bf16[16,7296]{1,0:T(8,128)(2,1)S(1)}, u32[]{:S(2)}, u32[]{:S(2)}) collective-permute-start(bf16[16,7296]{1,0:T(8,128)(2,1)S(1)} %pad_maximum_fusion.29), channel_id=1, source_target_pairs={{0,6},{1,7},{2,0},{3,1},{4,2},{5,3},{6,4},{7,5},{8,14},{9,15},{10,... | collective-permute-start | bytes 700424 | tf_op jit(solution)/shard_map/ppermute | solution.py:31
  193.4 9.7 %collective-permute-start.44 = (bf16[16,7296]{1,0:T(8,128)(2,1)S(1)}, bf16[16,7296]{1,0:T(8,128)(2,1)}, u32[]{:S(2)}, u32[]{:S(2)}) collective-permute-start(bf16[16,7296]{1,0:T(8,128)(2,1)S(1)} %fusion.14), channel_id=1, source_target_pairs={{0,1},{1,0},{2,3},{3,2},{4,5},{5,4},{6,7},{7,6},{8,9},{9,8},{10,11... | collective-permute-start | bytes 700424 | tf_op jit(solution)/shard_map/ppermute | solution.py:31
  203.1 23.4 %copy-start.14 = (f32[128,64]{1,0:T(8,128)S(1)}, f32[128,64]{1,0:T(8,128)}, u32[]{:S(2)}) copy-start(f32[128,64]{1,0:T(8,128)} %copy-done.13) | copy-start | bytes 98308
  203.1 24.0 %copy-start.5 = (bf16[128,7168]{1,0:T(8,128)(2,1)S(1)}, bf16[128,7168]{1,0:T(8,128)(2,1)}, u32[]{:S(2)}) copy-start(bf16[128,7168]{1,0:T(8,128)(2,1)} %param.15) | copy-start | bytes 5505028
  204.8 9.2 %collective-permute-start.48 = (bf16[16,128]{1,0:T(8,128)(2,1)S(1)}, bf16[16,128]{1,0:T(8,128)(2,1)S(1)}, u32[]{:S(2)}, u32[]{:S(2)}) collective-permute-start(bf16[16,128]{1,0:T(8,128)(2,1)S(1)} %slice.535), channel_id=1, source_target_pairs={{0,16},{1,17},{2,18},{3,19},{4,20},{5,21},{6,22},{7,23},{8,24},{9,... | collective-permute-start | bytes 12296 | tf_op jit(solution)/shard_map/ppermute | solution.py:31
  205.8 8.2 %collective-permute-start.49 = (bf16[16,128]{1,0:T(8,128)(2,1)S(1)}, bf16[16,128]{1,0:T(8,128)(2,1)S(1)}, u32[]{:S(2)}, u32[]{:S(2)}) collective-permute-start(bf16[16,128]{1,0:T(8,128)(2,1)S(1)} %slice.530), channel_id=1, source_target_pairs={{0,8},{1,9},{2,10},{3,11},{4,12},{5,13},{6,14},{7,15},{8,16},{9,17... | collective-permute-start | bytes 12296 | tf_op jit(solution)/shard_map/ppermute | solution.py:31
  207.8 13.2 %collective-permute-start.45 = (bf16[16,7168]{1,0:T(8,128)(2,1)S(1)}, bf16[16,7168]{1,0:T(8,128)(2,1)S(1)}, u32[]{:S(2)}, u32[]{:S(2)}) collective-permute-start(bf16[16,7168]{1,0:T(8,128)(2,1)S(1)} %slice.536), channel_id=1, source_target_pairs={{32,16},{33,17},{34,18},{35,19},{36,20},{37,21},{38,22},{39,23},{4... | collective-permute-start | bytes 688136 | tf_op jit(solution)/shard_map/ppermute | solution.py:38
  212.1 14.4 %collective-permute-start.46 = (bf16[16,7168]{1,0:T(8,128)(2,1)S(1)}, bf16[16,7168]{1,0:T(8,128)(2,1)S(1)}, u32[]{:S(2)}, u32[]{:S(2)}) collective-permute-start(bf16[16,7168]{1,0:T(8,128)(2,1)S(1)} %slice.531), channel_id=1, source_target_pairs={{32,8},{33,9},{34,10},{35,11},{36,12},{37,13},{38,14},{39,15},{40,... | collective-permute-start | bytes 688136 | tf_op jit(solution)/shard_map/ppermute | solution.py:38
  228.5 2.1 copy-start.1
  (18 other events, 22.0 us)
